TPU v7x, 32 devices: a whole 2x2x4 slice. The times are simulated.
32 devices in a mesh: fsdp: 4 (over y, x), ctx: 8 (over z, core).
Axes of the slice: x: 2, y: 2, z: 4, core: 2. Of those that a mesh axis runs over, the one named last changes fastest.
Arguments:
- inputs: bfloat16 [4, 2048, 768], P('fsdp', 'ctx'), may hold values from -6 to 6
- positions: int32 [4, 2048], P('fsdp', 'ctx'), may hold values from 0 to 2047, as said below
- in_weight: bfloat16 [768, 2304], P('fsdp'), may hold values from -0.21875 to 0.21875
- in_bias: bfloat16 [2304], P('fsdp'), may hold values from -0.3125 to 0.3125
- out_weight: bfloat16 [768, 768], P('fsdp'), may hold values from -0.109375 to 0.109375
- out_bias: bfloat16 [768], P('fsdp'), may hold values from -4 to 4
- up_weight: bfloat16 [768, 3072], P('fsdp'), may hold values from -0.21875 to 0.21875
- up_bias: bfloat16 [3072], P('fsdp'), may hold values from -6 to 6
- down_weight: bfloat16 [3072, 768], P('fsdp'), may hold values from -0.109375 to 0.109375
- down_bias: bfloat16 [768], P('fsdp'), may hold values from -4 to 4
- first_gain: bfloat16 [768], P('fsdp'), may hold values from 0.25 to 1.75
- first_shift: bfloat16 [768], P('fsdp'), may hold values from -4 to 4
- second_gain: bfloat16 [768], P('fsdp'), may hold values from 0.25 to 1.75
- second_shift: bfloat16 [768], P('fsdp'), may hold values from -4 to 4
- out_grad: bfloat16 [4, 2048, 768], P('fsdp', 'ctx'), may hold values from -6 to 6
Outputs:
- output: bfloat16 [4, 2048, 768], P('fsdp', 'ctx')
- input_gradient: float32 [4, 2048, 768], P('fsdp', 'ctx')
- in_weight_gradient: float32 [768, 2304], P('fsdp')
- in_bias_gradient: float32 [2304], P('fsdp')
- out_weight_gradient: float32 [768, 768], P('fsdp')
- out_bias_gradient: float32 [768], P('fsdp')
- up_weight_gradient: float32 [768, 3072], P('fsdp')
- up_bias_gradient: float32 [3072], P('fsdp')
- down_weight_gradient: float32 [3072, 768], P('fsdp')
- down_bias_gradient: float32 [768], P('fsdp')
- first_gain_gradient: float32 [768], P('fsdp')
- first_shift_gradient: float32 [768], P('fsdp')
- second_gain_gradient: float32 [768], P('fsdp')
- second_shift_gradient: float32 [768], P('fsdp')
Inputs may be any that keep to these rules, and one draw needn't show every extreme that they name: Each row holds every position of its sequence once, in runs of 128 consecutive rising positions that start at multiples of 128; the order of the runs differs from row to row.
All inputs are finite; a program needn't handle non-finite values.
Results may differ from a plain program's by a relative error of at most 0.018.
Values may be sent and summed in bfloat16 or wider, within the bound.
No kernel may reach another device: no remote copies, remote signals or barrier semaphores. Data moves between devices by JAX's collectives and lax.ppermute only.
A program may use at most 192 MiB of HBM per device.

v0:
```python
import math
import jax
import jax.numpy as jnp
from jax import lax
from jax.sharding import PartitionSpec as P

HEAD = 64
ROT = 16
NEG = -1e30
EPS = 1e-05


def from_behind(x, axis, by):
    size = lax.axis_size(axis)
    return lax.ppermute(x, axis, [(i, (i + by) % size) for i in range(size)])


def layer_norm(values, gain, shift):
    mean = jnp.mean(values, -1, keepdims=True)
    centred = values - mean
    spread = jnp.mean(centred * centred, -1, keepdims=True)
    return centred * lax.rsqrt(spread + EPS) * gain + shift


def turn_tables(positions):
    ladder = 10000.0 ** (-jnp.arange(0, ROT, 2, dtype=jnp.float32) / ROT)
    angle = positions.astype(jnp.float32)[..., None] * ladder
    angle = jnp.concatenate([angle, angle], -1)
    return (jnp.cos(angle), jnp.sin(angle))


def rotate(values, cosine, sine):
    half = ROT // 2
    part = values[..., :ROT]
    turned = jnp.concatenate([-part[..., half:], part[..., :half]], -1)
    part = part * cosine[..., None, :] + turned * sine[..., None, :]
    return jnp.concatenate([part, values[..., ROT:]], -1)


def across(left, right):
    return lax.dot_general(
        left, right, (((0,), (0,)), ((), ())), preferred_element_type=jnp.float32
    )


def against(left, right):
    return lax.dot_general(
        left, right, (((1,), (1,)), ((), ())), preferred_element_type=jnp.float32
    )


def softmax_step(carry, queries, query_pos, keys, values, key_pos, scale):
    peak, total, summed = carry
    scores = jnp.einsum("qhd,khd->hqk", queries, keys, preferred_element_type=jnp.float32) * scale
    allowed = (key_pos[None, :] <= query_pos[:, None])[None]
    new_peak = jnp.maximum(peak, jnp.max(jnp.where(allowed, scores, NEG), -1))
    weights = jnp.where(allowed, jnp.exp(scores - new_peak[..., None]), 0.0)
    fade = jnp.exp(peak - new_peak)
    total = total * fade + jnp.sum(weights, -1)
    added = jnp.einsum(
        "hqk,khd->qhd", weights.astype(jnp.bfloat16), values, preferred_element_type=jnp.float32
    )
    summed = summed * jnp.transpose(fade)[:, :, None] + added
    return (new_peak, total, summed)


def gradient_step(
    state, queries, query_pos, outs_back, log_total, spread, keys, values, key_pos, scale
):
    back_query, back_key, back_value = state
    scores = jnp.einsum("qhd,khd->hqk", queries, keys, preferred_element_type=jnp.float32) * scale
    allowed = (key_pos[None, :] <= query_pos[:, None])[None]
    probs = jnp.where(allowed, jnp.exp(scores - log_total[..., None]), 0.0)
    back_probs = jnp.einsum("qhd,khd->hqk", outs_back, values, preferred_element_type=jnp.float32)
    back_scores = (probs * (back_probs - spread[..., None])).astype(jnp.bfloat16)
    back_query = (
        back_query
        + jnp.einsum("hqk,khd->qhd", back_scores, keys, preferred_element_type=jnp.float32) * scale
    )
    back_key = (
        back_key
        + jnp.einsum("hqk,qhd->khd", back_scores, queries, preferred_element_type=jnp.float32)
        * scale
    )
    back_value = back_value + jnp.einsum(
        "hqk,qhd->khd", probs.astype(jnp.bfloat16), outs_back, preferred_element_type=jnp.float32
    )
    return (back_query, back_key, back_value)


def on_device(
    inputs,
    positions,
    in_weight,
    in_bias,
    out_weight,
    out_bias,
    up_weight,
    up_bias,
    down_weight,
    down_bias,
    first_gain,
    first_shift,
    second_gain,
    second_shift,
    out_grad,
):
    gathered = (
        lax.all_gather(in_weight, "fsdp", axis=0, tiled=True),
        lax.all_gather(in_bias, "fsdp", axis=0, tiled=True),
        lax.all_gather(out_weight, "fsdp", axis=0, tiled=True),
        lax.all_gather(out_bias, "fsdp", axis=0, tiled=True),
        lax.all_gather(up_weight, "fsdp", axis=0, tiled=True),
        lax.all_gather(up_bias, "fsdp", axis=0, tiled=True),
        lax.all_gather(down_weight, "fsdp", axis=0, tiled=True),
        lax.all_gather(down_bias, "fsdp", axis=0, tiled=True),
        lax.all_gather(first_gain, "fsdp", axis=0, tiled=True),
        lax.all_gather(first_shift, "fsdp", axis=0, tiled=True),
        lax.all_gather(second_gain, "fsdp", axis=0, tiled=True),
        lax.all_gather(second_shift, "fsdp", axis=0, tiled=True),
    )
    (
        full_in,
        full_in_bias,
        full_out,
        full_out_bias,
        full_up,
        full_up_bias,
        full_down,
        full_down_bias,
        gain_one,
        shift_one,
        gain_two,
        shift_two,
    ) = gathered
    tokens = inputs.shape[1]
    width = inputs.shape[2]
    heads = width // HEAD
    scale = 1.0 / math.sqrt(HEAD)
    query_pos = positions[0]
    all_pos = lax.all_gather(query_pos, "ctx", axis=0, tiled=True)
    resid = inputs[0].astype(jnp.float32)

    def norms(values, gain_a, shift_a, gain_b, shift_b):
        return (layer_norm(values, gain_a, shift_a), layer_norm(values, gain_b, shift_b))

    (normed_one, normed_two), norm_back = jax.vjp(
        norms,
        resid,
        gain_one.astype(jnp.float32),
        shift_one.astype(jnp.float32),
        gain_two.astype(jnp.float32),
        shift_two.astype(jnp.float32),
    )
    first = normed_one.astype(jnp.bfloat16)
    second = normed_two.astype(jnp.bfloat16)
    projected = jnp.dot(first, full_in, preferred_element_type=jnp.float32) + full_in_bias.astype(
        jnp.float32
    )
    projected = projected.reshape(tokens, 3, heads, HEAD)
    cosine, sine = turn_tables(query_pos)
    queries = rotate(projected[:, 0], cosine, sine).astype(jnp.bfloat16)
    keys = rotate(projected[:, 1], cosine, sine).astype(jnp.bfloat16)
    values = projected[:, 2].astype(jnp.bfloat16)
    start_state = (
        jnp.full((heads, tokens), NEG, jnp.float32),
        jnp.zeros((heads, tokens), jnp.float32),
        jnp.zeros((tokens, heads, HEAD), jnp.float32),
    )
    carry = start_state
    key_piece = lax.all_gather(keys, "ctx", axis=0, tiled=True)
    value_piece = lax.all_gather(values, "ctx", axis=0, tiled=True)
    count = key_piece.shape[0]
    size = 512

    def one_block(inner, offset):
        key_block = lax.dynamic_slice_in_dim(key_piece, offset, size, 0)
        value_block = lax.dynamic_slice_in_dim(value_piece, offset, size, 0)
        key_pos = lax.dynamic_slice_in_dim(all_pos, offset, size, 0)
        result = softmax_step(inner, queries, query_pos, key_block, value_block, key_pos, scale)
        return (result, None)

    carry, _ = lax.scan(one_block, carry, jnp.arange(0, count, size, dtype=jnp.int32))
    peak, total, summed = carry
    attended = summed / jnp.transpose(total)[:, :, None]
    log_total = peak + jnp.log(total)
    mixed = attended.reshape(tokens, width).astype(jnp.bfloat16)
    up = jnp.dot(second, full_up, preferred_element_type=jnp.float32) + full_up_bias.astype(
        jnp.float32
    )
    activated, gelu_back = jax.vjp(lambda value: jax.nn.gelu(value, approximate=False), up)
    activated = activated.astype(jnp.bfloat16)
    branch_attn = jnp.dot(
        mixed, full_out, preferred_element_type=jnp.float32
    ) + full_out_bias.astype(jnp.float32)
    branch_ff = jnp.dot(
        activated, full_down, preferred_element_type=jnp.float32
    ) + full_down_bias.astype(jnp.float32)
    output = resid + branch_attn + branch_ff
    cotangent = out_grad[0]
    back_out = cotangent.astype(jnp.float32)
    bias_sum = jnp.sum(back_out, 0)
    out_weight_part = across(mixed, cotangent)
    down_weight_part = across(activated, cotangent)
    back_mixed = against(cotangent, full_out).astype(jnp.bfloat16)
    back_active = against(cotangent, full_down)
    back_up = gelu_back(back_active)[0].astype(jnp.bfloat16)
    up_weight_part = across(second, back_up)
    up_bias_part = jnp.sum(back_up.astype(jnp.float32), 0)
    back_second = against(back_up, full_up)
    outs_back = back_mixed.reshape(tokens, heads, HEAD)
    spread = jnp.einsum("qhd,qhd->hq", outs_back.astype(jnp.float32), attended)
    cycle_size = lax.axis_size("ctx")
    here = lax.axis_index("ctx")
    zeros = jnp.zeros((tokens, heads, HEAD), jnp.float32)

    def key_turn(turn, state):
        moving_key, moving_value, back_key, back_value, back_query = state
        owner = (here - turn) % cycle_size
        key_pos = lax.dynamic_slice_in_dim(all_pos, owner * tokens, tokens, 0)
        back_query, back_key, back_value = gradient_step(
            (back_query, back_key, back_value),
            queries,
            query_pos,
            outs_back,
            log_total,
            spread,
            moving_key,
            moving_value,
            key_pos,
            scale,
        )
        moving_key, moving_value = from_behind((moving_key, moving_value), "ctx", 1)
        back_key, back_value = (
            from_behind(back_key.astype(jnp.bfloat16), "ctx", 1).astype(back_key.dtype),
            from_behind(back_value.astype(jnp.bfloat16), "ctx", 1).astype(back_value.dtype),
        )
        return (moving_key, moving_value, back_key, back_value, back_query)

    final = lax.fori_loop(0, cycle_size, key_turn, (keys, values, zeros, zeros, zeros))
    back_query, back_key, back_value = (final[4], final[2], final[3])
    back_query = rotate(back_query, cosine, -sine)
    back_key = rotate(back_key, cosine, -sine)
    back_projected = (
        jnp.stack([back_query, back_key, back_value], 1)
        .reshape(tokens, 3 * width)
        .astype(jnp.bfloat16)
    )
    in_weight_part = across(first, back_projected)
    in_bias_part = jnp.sum(back_projected.astype(jnp.float32), 0)
    back_first = against(back_projected, full_in)
    back_resid, gain_one_part, shift_one_part, gain_two_part, shift_two_part = norm_back(
        (back_first, back_second)
    )
    input_gradient = back_out + back_resid
    shares = (
        lax.psum_scatter(
            in_weight_part.astype(jnp.bfloat16), "fsdp", scatter_dimension=0, tiled=True
        ).astype(jnp.float32),
        lax.psum_scatter(
            in_bias_part.astype(jnp.bfloat16), "fsdp", scatter_dimension=0, tiled=True
        ).astype(jnp.float32),
        lax.psum_scatter(
            out_weight_part.astype(jnp.bfloat16), "fsdp", scatter_dimension=0, tiled=True
        ).astype(jnp.float32),
        lax.psum_scatter(
            bias_sum.astype(jnp.bfloat16), "fsdp", scatter_dimension=0, tiled=True
        ).astype(jnp.float32),
        lax.psum_scatter(
            up_weight_part.astype(jnp.bfloat16), "fsdp", scatter_dimension=0, tiled=True
        ).astype(jnp.float32),
        lax.psum_scatter(
            up_bias_part.astype(jnp.bfloat16), "fsdp", scatter_dimension=0, tiled=True
        ).astype(jnp.float32),
        lax.psum_scatter(
            down_weight_part.astype(jnp.bfloat16), "fsdp", scatter_dimension=0, tiled=True
        ).astype(jnp.float32),
        lax.psum_scatter(
            gain_one_part.astype(jnp.bfloat16), "fsdp", scatter_dimension=0, tiled=True
        ).astype(jnp.float32),
        lax.psum_scatter(
            shift_one_part.astype(jnp.bfloat16), "fsdp", scatter_dimension=0, tiled=True
        ).astype(jnp.float32),
        lax.psum_scatter(
            gain_two_part.astype(jnp.bfloat16), "fsdp", scatter_dimension=0, tiled=True
        ).astype(jnp.float32),
        lax.psum_scatter(
            shift_two_part.astype(jnp.bfloat16), "fsdp", scatter_dimension=0, tiled=True
        ).astype(jnp.float32),
    )
    totals = (
        lax.psum(shares[0].astype(jnp.bfloat16), "ctx").astype(jnp.float32),
        lax.psum(shares[1].astype(jnp.bfloat16), "ctx").astype(jnp.float32),
        lax.psum(shares[2].astype(jnp.bfloat16), "ctx").astype(jnp.float32),
        lax.psum(shares[3].astype(jnp.bfloat16), "ctx").astype(jnp.float32),
        lax.psum(shares[4].astype(jnp.bfloat16), "ctx").astype(jnp.float32),
        lax.psum(shares[5].astype(jnp.bfloat16), "ctx").astype(jnp.float32),
        lax.psum(shares[6].astype(jnp.bfloat16), "ctx").astype(jnp.float32),
        lax.psum(shares[7].astype(jnp.bfloat16), "ctx").astype(jnp.float32),
        lax.psum(shares[8].astype(jnp.bfloat16), "ctx").astype(jnp.float32),
        lax.psum(shares[9].astype(jnp.bfloat16), "ctx").astype(jnp.float32),
        lax.psum(shares[10].astype(jnp.bfloat16), "ctx").astype(jnp.float32),
    )
    return (
        output.astype(jnp.bfloat16)[None],
        input_gradient[None],
        totals[0],
        totals[1],
        totals[2],
        totals[3],
        totals[4],
        totals[5],
        totals[6],
        totals[3],
        totals[7],
        totals[8],
        totals[9],
        totals[10],
    )


def solution(mesh):
    return jax.shard_map(
        on_device,
        mesh=mesh,
        in_specs=(
            P("fsdp", "ctx", None),
            P("fsdp", "ctx"),
            P("fsdp", None),
            P("fsdp"),
            P("fsdp", None),
            P("fsdp"),
            P("fsdp", None),
            P("fsdp"),
            P("fsdp", None),
            P("fsdp"),
            P("fsdp"),
            P("fsdp"),
            P("fsdp"),
            P("fsdp"),
            P("fsdp", "ctx", None),
        ),
        out_specs=(
            P("fsdp", "ctx", None),
            P("fsdp", "ctx", None),
            P("fsdp", None),
            P("fsdp"),
            P("fsdp", None),
            P("fsdp"),
            P("fsdp", None),
            P("fsdp"),
            P("fsdp", None),
            P("fsdp"),
            P("fsdp"),
            P("fsdp"),
            P("fsdp"),
            P("fsdp"),
        ),
        check_vma=False,
    )
```

profile of v0, /device:TPU:0, one launch (start us, length us, event | category | flops | bytes accessed | tf_op | source)
XLA Modules:
  0.0 707.0 jit_solution(10681487738134994407)
XLA Ops:
  14.8 18.4 %all-reduce.17 = (bf16[768]{0:T(1024)(128)(2,1)}, bf16[768]{0:T(1024)(128)(2,1)}, bf16[2304]{0:T(1024)(128)(2,1)S(1)}, bf16[768]{0:T(1024)(128)(2,1)S(1)}, bf16[768]{0:T(1024)(128)(2,1)S(1)}) all-reduce(bf16[768]{0:T(1024)(128)(2,1)S(1)} %dynamic-update-slice.5, ...), channel_id=1, replica_groups=mesh['fsdp'=4,'ctx'=8] {'fsdp'}, use_global_device_ids=true, to_apply=%add.5 | all-reduce | flops 5376 | bytes 21504
  37.1 22.8 %all-gather.10.cloned.1.call-done = bf16[768,2304]{1,0:T(8,128)(2,1)} async-done(((bf16[192,2304]{1,0:T(8,128)(2,1)}), bf16[768,2304]{1,0:T(8,128)(2,1)}) %all-gather.10.cloned.1.call-update) | async-done | bytes 3538960 | tf_op jit(solution)/shard_map/all_gather | solution.py:109
  59.9 4.7 convolution_add_fusion
  71.0 12.8 %all-gather = s32[1,2048]{1,0:T(1,128)} all-gather(s32[1,256]{1,0:T(1,128)} %param.20), channel_id=2, replica_groups=mesh['fsdp'=4,'ctx'=8] {'ctx'}, dimensions={1}, use_global_device_ids=true | all-gather | bytes 9216 | tf_op jit(solution)/shard_map/all_gather | solution.py:141
  85.9 8.1 %all-gather.2 = bf16[4,1,768]{2,1,0:T(2,128)(2,1)S(1)} all-gather(bf16[1,1,768]{2,1,0:T(2,128)(2,1)S(1)} %reshape.293), channel_id=1, replica_groups=mesh['fsdp'=4,'ctx'=8] {'fsdp'}, dimensions={0}, use_global_device_ids=true | all-gather | bytes 7680 | tf_op jit(solution)/shard_map/all_gather | solution.py:114
  94.1 13.7 %all-gather.12.cloned.1.call-done = bf16[2048,12,64]{0,2,1:T(8,128)(2,1)} async-done(((bf16[256,12,64]{0,2,1:T(8,128)(2,1)}), bf16[2048,12,64]{0,2,1:T(8,128)(2,1)}) %all-gather.12.cloned.1.call-update) | async-done | bytes 3145744 | tf_op jit(solution)/shard_map/all_gather | solution.py:171
  107.7 41.4 %all-gather.20.cloned.1.call-done = bf16[2048,1,12,64]{0,3,2,1:T(8,128)(2,1)} async-done(((bf16[256,1,12,64]{0,3,2,1:T(8,128)(2,1)}), bf16[2048,1,12,64]{0,3,2,1:T(8,128)(2,1)}) %all-gather.20.cloned.1.call-update) | async-done | bytes 3145744 | tf_op jit(solution)/shard_map/all_gather | solution.py:172
  149.1 64.1 %while.39 = (s32[]{:T(128)}, f32[12,256]{1,0:T(8,128)S(1)}, f32[12,256]{1,0:T(8,128)S(1)}, f32[256,12,64]{0,2,1:T(8,128)S(1)}, s32[4]{0:T(128)S(1)}, /*index=5*/...) while((s32[]{:T(128)}, f32[12,256]{1,0:T(8,128)S(1)}, ...), condition=%wide.region_5.6_spmd.clone, body=%wide.region_2.5_spmd.clone.sunk | while | flops 420694016 | bytes 48307420 | solution.py:183
  153.2 5.7 fusion.173
  158.9 4.8 fusion.177
  169.2 5.5 fusion.173
  174.7 4.8 fusion.177
  185.8 5.5 fusion.173
  191.3 4.8 fusion.177
  201.6 5.4 fusion.173
  207.1 4.7 fusion.177
  215.2 11.6 %multiply_convert_fusion.1 = (bf16[256,3072]{1,0:T(8,128)(2,1)S(1)}, f32[256,3072]{1,0:T(8,128)}, f32[256,3072]{1,0:T(8,128)}) fusion(f32[3072]{0:T(1024)S(1)} %bitcast.232, bf16[768,3072]{1,0:T(8,128)(2,1)} %all-gather.16.cloned.1.call-done, bf16[1,256,768]{2,1,0:T(8,128)(2,1)S(1)} %copy-done.3, f32[768]{0:T(1024)S(1)} %convert_element_type.251, ...), kind=kOutput, calls=%fused_computation.54 | convolution fusion | flops 1261043712 | bytes 12996608 | tf_op jit(solution)/shard_map/dot_general | solution.py:188
  226.7 38.2 %all-gather.18.cloned.1.call-done = bf16[3072,768]{1,0:T(8,128)(2,1)} async-done(((bf16[768,768]{1,0:T(8,128)(2,1)}), bf16[3072,768]{1,0:T(8,128)(2,1)}) %all-gather.18.cloned.1.call-update) | async-done | bytes 4718608 | tf_op jit(solution)/shard_map/all_gather | solution.py:115
  264.9 6.8 fusion.119
  272.9 3.7 convolution_convert_fusion.1
  276.7 17.6 %all-gather.14.cloned.1.call-done = bf16[768,768]{1,0:T(8,128)(2,1)} async-done(((bf16[192,768]{1,0:T(8,128)(2,1)}), bf16[768,768]{1,0:T(8,128)(2,1)}) %all-gather.14.cloned.1.call-update) | async-done | bytes 1179664 | tf_op jit(solution)/shard_map/all_gather | solution.py:111
  294.4 2.5 convolution_convert_fusion.4
  300.7 3.5 convolution_convert_fusion
  307.7 244.7 %while.40 = (s32[]{:T(128)}, bf16[256,12,64]{0,2,1:T(8,128)(2,1)}, bf16[256,12,64]{0,2,1:T(8,128)(2,1)}, f32[256,12,64]{0,2,1:T(8,128)S(1)}, f32[256,12,64]{0,2,...) while((s32[]{:T(128)}, bf16[256,12,64]{0,2,1:T(8,128)(2,1)}, ...), condition=%wide.region_9.10_spmd.clone, body=%wide.region_8.9_spmd.clone.sunk | while | flops 513605632 | bytes 40837772 | solution.py:240
  316.4 2.6 fusion.190
  326.8 3.1 collective-permute-done.3
  334.1 4.2 collective-permute-done.1
  346.9 2.6 fusion.190
  352.6 3.6 collective-permute-done.2
  357.3 3.1 collective-permute-done.3
  364.7 4.2 collective-permute-done.1
  377.6 2.6 fusion.190
  381.9 5.1 collective-permute-done.2
  388.0 3.1 collective-permute-done.3
  395.4 4.2 collective-permute-done.1
  404.6 2.5 multiply_convert_fusion.3
  408.2 2.7 fusion.190
  412.6 5.0 collective-permute-done.2
  418.6 3.1 collective-permute-done.3
  426.0 4.2 collective-permute-done.1
  438.8 2.6 fusion.190
  443.1 5.1 collective-permute-done.2
  449.2 3.1 collective-permute-done.3
  456.6 4.2 collective-permute-done.1
  469.4 2.6 fusion.190
  473.6 5.1 collective-permute-done.2
  479.8 3.1 collective-permute-done.3
  487.1 4.2 collective-permute-done.1
  499.9 2.6 fusion.190
  504.2 5.1 collective-permute-done.2
  510.3 3.1 collective-permute-done.3
  517.7 4.2 collective-permute-done.1
  530.5 2.6 fusion.190
  534.7 5.1 collective-permute-done.2
  540.9 3.1 collective-permute-done.3
  548.2 4.2 collective-permute-done.1
  556.2 3.2 convolution_convert_fusion.2
  563.0 4.8 fusion.121
  570.0 34.4 %reduce-scatter.5.cloned.1.call-done = bf16[192,2304]{1,0:T(8,128)(2,1)} async-done(((bf16[768,2304]{1,0:T(8,128)(2,1)}), bf16[192,2304]{1,0:T(8,128)(2,1)}) %reduce-scatter.5.cloned.1.call-update) | async-done | bytes 884752 | tf_op jit(solution)/shard_map/reduce_scatter | solution.py:257
  606.4 15.3 %all-reduce.16 = (bf16[768]{0:T(1024)(128)(2,1)S(1)}, bf16[768]{0:T(1024)(128)(2,1)S(1)}, bf16[2304]{0:T(1024)(128)(2,1)S(1)}, bf16[768]{0:T(1024)(128)(2,1)S(1)...) all-reduce(bf16[768]{0:T(1024)(128)(2,1)S(1)} %dynamic-update-slice, ...), channel_id=1, replica_groups=mesh['fsdp'=4,'ctx'=8] {'fsdp'}, use_global_device_ids=true, to_apply=%add.6 | all-reduce | flops 10752 | bytes 43008
  622.3 15.3 %all-reduce.14 = (bf16[576]{0:T(1024)(128)(2,1)S(1)}, bf16[192]{0:T(256)(128)(2,1)S(1)}, bf16[768]{0:T(1024)(128)(2,1)S(1)}, bf16[192]{0:T(256)(128)(2,1)S(1)}, ...) all-reduce(bf16[576]{0:T(1024)(128)(2,1)S(1)} %dynamic-slice.8, ...), channel_id=1, replica_groups=mesh['fsdp'=4,'ctx'=8] {'ctx'}, use_global_device_ids=true, to_apply=%region_16.17 | all-reduce | flops 2304 | bytes 9216 | tf_op jit(solution)/shard_map/psum | solution.py:293
  641.1 3.9 convolution_add_fusion.3
  647.7 45.3 %all-reduce.20.cloned.1.call-done = (bf16[192,2304]{1,0:T(8,128)(2,1)}, bf16[192,768]{1,0:T(8,128)(2,1)}, bf16[192,3072]{1,0:T(8,128)(2,1)}, bf16[768,768]{1,0:T(8,128)(2,1)}) async-done(((bf16[192,2304]{1,0:T(8,128)(2,1)}, bf16[192,768]{1,0:T(8,128)(2,1)}, bf16[192,3072]{1,0:T(8,128)(2,1)}, bf16[768,768]{1,0:T(8,128)(2,1)}), (bf16[192,2304]{1,0:T(8,128)(2,1)}, bf16[192,768]{1,0:T(8,128)(2,1)}, ...) | async-done | bytes 3538960 | tf_op jit(solution)/shard_map/psum | solution.py:292
  693.0 3.1 convert_element_type.271
  (434 shorter events, 191.8 us)
Async XLA Ops:
  7.2 52.8 %all-gather.10.cloned.1.call-start = ((), (), s32[]{:S(2)}) async-start(), calls=%async_computation.4 | async-start | bytes 4423680 | tf_op jit(solution)/shard_map/all_gather | solution.py:109
  7.9 99.8 %all-gather.12.cloned.1.call-start = ((), (), s32[]{:S(2)}) async-start(), calls=%async_computation.5 | async-start | bytes 3538944 | tf_op jit(solution)/shard_map/all_gather | solution.py:171
  33.2 31.4 %copy-start.23 = (f32[768]{0:T(1024)}, f32[768]{0:T(1024)S(1)}, u32[]{:S(2)}) copy-start(f32[768]{0:T(1024)S(1)} %convert_element_type.241) | copy-start | bytes 9220
  33.2 31.4 %copy-start.29 = (f32[768]{0:T(1024)}, f32[768]{0:T(1024)S(1)}, u32[]{:S(2)}) copy-start(f32[768]{0:T(1024)S(1)} %convert_element_type.242) | copy-start | bytes 9220
  34.7 32.3 %copy-start.27 = (f32[256,16]{0,1:T(8,128)}, f32[256,16]{0,1:T(8,128)S(1)}, u32[]{:S(2)}) copy-start(f32[256,16]{0,1:T(8,128)S(1)} %get-tuple-element.582) | copy-start | bytes 49156
  35.8 28.8 %copy-start.32 = (f32[256]{0:T(256)}, f32[256]{0:T(256)S(1)}, u32[]{:S(2)}) copy-start(f32[256]{0:T(256)S(1)} %broadcast_multiply_fusion.1) | copy-start | bytes 3076
  37.1 27.6 %copy-start.40 = (f32[256]{0:T(256)}, f32[256]{0:T(256)S(1)}, u32[]{:S(2)}) copy-start(f32[256]{0:T(256)S(1)} %fusion.73) | copy-start | bytes 3076
  37.1 27.6 %copy-start.35 = (f32[256]{0:T(256)}, f32[256]{0:T(256)S(1)}, u32[]{:S(2)}) copy-start(f32[256]{0:T(256)S(1)} %fusion.108) | copy-start | bytes 3076
  68.4 80.7 %all-gather.20.cloned.1.call-start = ((), (), s32[]{:S(2)}) async-start(), calls=%async_computation.13 | async-start | bytes 3538944 | tf_op jit(solution)/shard_map/all_gather | solution.py:172
  69.2 145.9 %all-gather.16.cloned.1.call-start = ((), (), s32[]{:S(2)}) async-start(), calls=%async_computation.7 | async-start | bytes 5898240 | tf_op jit(solution)/shard_map/all_gather | solution.py:113
  69.8 195.1 %all-gather.18.cloned.1.call-start = ((), (), s32[]{:S(2)}) async-start(), calls=%async_computation.8 | async-start | bytes 5898240 | tf_op jit(solution)/shard_map/all_gather | solution.py:115
  70.4 223.9 %all-gather.14.cloned.1.call-start = ((), (), s32[]{:S(2)}) async-start(), calls=%async_computation.6 | async-start | bytes 1474560 | tf_op jit(solution)/shard_map/all_gather | solution.py:111
  71.0 499.0 %reduce-scatter.7.cloned.1.call-start = ((), (), s32[]{:S(2)}) async-start(), calls=%async_computation.10 | async-start | bytes 1474560 | tf_op jit(solution)/shard_map/reduce_scatter | solution.py:263
  84.5 187.2 %copy-start.25 = (f32[768]{0:T(1024)}, f32[768]{0:T(1024)S(1)}, u32[]{:S(2)}) copy-start(f32[768]{0:T(1024)S(1)} %convert_element_type.250) | copy-start | bytes 9220
  149.1 64.3 %copy-start.4 = (bf16[1,256,768]{2,1,0:T(8,128)(2,1)S(1)}, bf16[1,256,768]{2,1,0:T(8,128)(2,1)}, u32[]{:S(2)}) copy-start(bf16[1,256,768]{2,1,0:T(8,128)(2,1)} %param.33) | copy-start | bytes 1179652
  158.9 4.9 copy-start
  174.7 5.7 copy-start
  191.3 4.9 copy-start
  207.0 4.8 copy-start
  213.2 13.5 %copy-start.17 = (f32[12,256]{1,0:T(8,128)}, f32[12,256]{1,0:T(8,128)S(1)}, u32[]{:S(2)}) copy-start(f32[12,256]{1,0:T(8,128)S(1)} %get-tuple-element.380) | copy-start | bytes 36868
  213.3 13.4 %copy-start.8 = (bf16[256,12,64]{0,2,1:T(8,128)(2,1)}, bf16[256,12,64]{0,2,1:T(8,128)(2,1)S(1)}, u32[]{:S(2)}) copy-start(bf16[256,12,64]{0,2,1:T(8,128)(2,1)S(1)} %fusion.99) | copy-start | bytes 1179652
  214.9 355.1 %reduce-scatter.9.cloned.1.call-start = ((), (), s32[]{:S(2)}) async-start(), calls=%async_computation.11 | async-start | bytes 5898240 | tf_op jit(solution)/shard_map/reduce_scatter | solution.py:269
  226.7 74.0 %copy-start.10 = (bf16[256,3072]{1,0:T(8,128)(2,1)}, bf16[256,3072]{1,0:T(8,128)(2,1)S(1)}, u32[]{:S(2)}) copy-start(bf16[256,3072]{1,0:T(8,128)(2,1)S(1)} %get-tuple-element.560) | copy-start | bytes 4718596
  276.6 293.4 %reduce-scatter.11.cloned.1.call-start = ((), (), s32[]{:S(2)}) async-start(), calls=%async_computation.12 | async-start | bytes 5898240 | tf_op jit(solution)/shard_map/reduce_scatter | solution.py:275
  304.3 300.2 %reduce-scatter.5.cloned.1.call-start = ((), (), s32[]{:S(2)}) async-start(), calls=%async_computation.9 | async-start | bytes 4423680 | tf_op jit(solution)/shard_map/reduce_scatter | solution.py:257
  307.7 247.0 %copy-start.28 = (f32[256,16]{0,1:T(8,128)S(1)}, f32[256,16]{0,1:T(8,128)}, u32[]{:S(2)}) copy-start(f32[256,16]{0,1:T(8,128)} %copy-done.27) | copy-start | bytes 49156
  316.4 5.8 copy-start.1
  316.4 9.3 %collective-permute-start.2 = (bf16[256,12,64]{0,2,1:T(8,128)(2,1)}, bf16[256,12,64]{0,2,1:T(8,128)(2,1)}, u32[]{:S(2)}, u32[]{:S(2)}) collective-permute-start(bf16[256,12,64]{0,2,1:T(8,128)(2,1)} %fusion.189), channel_id=1, source_target_pairs={{0,1},{1,2},{2,3},{3,4},{4,5},{5,6},{6,7},{7,0},{8,9},{9,10},{10,1... | collective-permute-start | bytes 1179656 | tf_op jit(solution)/shard_map/while/body/eval_jaxpr/ppermute | solution.py:15
  319.0 10.9 %collective-permute-start.3 = (bf16[256,12,64]{0,2,1:T(8,128)(2,1)}, bf16[256,12,64]{0,2,1:T(8,128)(2,1)}, u32[]{:S(2)}, u32[]{:S(2)}) collective-permute-start(bf16[256,12,64]{0,2,1:T(8,128)(2,1)} %fusion.190), channel_id=1, source_target_pairs={{0,1},{1,2},{2,3},{3,4},{4,5},{5,6},{6,7},{7,0},{8,9},{9,10},{10,1... | collective-permute-start | bytes 1179656 | tf_op jit(solution)/shard_map/while/body/eval_jaxpr/ppermute | solution.py:15
  320.5 13.6 %collective-permute-start = (bf16[256,12,64]{0,2,1:T(8,128)(2,1)S(1)}, bf16[256,12,64]{0,2,1:T(8,128)(2,1)}, u32[]{:S(2)}, u32[]{:S(2)}) collective-permute-start(bf16[256,12,64]{0,2,1:T(8,128)(2,1)S(1)} %copy.76), channel_id=1, source_target_pairs={{0,1},{1,2},{2,3},{3,4},{4,5},{5,6},{6,7},{7,0},{8,9},{9,10},{10,1... | collective-permute-start | bytes 1179656 | tf_op jit(solution)/shard_map/while/body/eval_jaxpr/ppermute | solution.py:15
  320.6 17.7 %collective-permute-start.1 = (bf16[256,12,64]{0,2,1:T(8,128)(2,1)}, bf16[256,12,64]{0,2,1:T(8,128)(2,1)}, u32[]{:S(2)}, u32[]{:S(2)}) collective-permute-start(bf16[256,12,64]{0,2,1:T(8,128)(2,1)} %copy.77), channel_id=1, source_target_pairs={{0,1},{1,2},{2,3},{3,4},{4,5},{5,6},{6,7},{7,0},{8,9},{9,10},{10,1... | collective-permute-start | bytes 1179656 | tf_op jit(solution)/shard_map/while/body/eval_jaxpr/ppermute | solution.py:15
  346.9 9.3 %collective-permute-start.2 = (bf16[256,12,64]{0,2,1:T(8,128)(2,1)}, bf16[256,12,64]{0,2,1:T(8,128)(2,1)}, u32[]{:S(2)}, u32[]{:S(2)}) collective-permute-start(bf16[256,12,64]{0,2,1:T(8,128)(2,1)} %fusion.189), channel_id=1, source_target_pairs={{0,1},{1,2},{2,3},{3,4},{4,5},{5,6},{6,7},{7,0},{8,9},{9,10},{10,1... | collective-permute-start | bytes 1179656 | tf_op jit(solution)/shard_map/while/body/eval_jaxpr/ppermute | solution.py:15
  349.6 10.9 %collective-permute-start.3 = (bf16[256,12,64]{0,2,1:T(8,128)(2,1)}, bf16[256,12,64]{0,2,1:T(8,128)(2,1)}, u32[]{:S(2)}, u32[]{:S(2)}) collective-permute-start(bf16[256,12,64]{0,2,1:T(8,128)(2,1)} %fusion.190), channel_id=1, source_target_pairs={{0,1},{1,2},{2,3},{3,4},{4,5},{5,6},{6,7},{7,0},{8,9},{9,10},{10,1... | collective-permute-start | bytes 1179656 | tf_op jit(solution)/shard_map/while/body/eval_jaxpr/ppermute | solution.py:15
  349.6 15.1 %collective-permute-start = (bf16[256,12,64]{0,2,1:T(8,128)(2,1)S(1)}, bf16[256,12,64]{0,2,1:T(8,128)(2,1)}, u32[]{:S(2)}, u32[]{:S(2)}) collective-permute-start(bf16[256,12,64]{0,2,1:T(8,128)(2,1)S(1)} %copy.76), channel_id=1, source_target_pairs={{0,1},{1,2},{2,3},{3,4},{4,5},{5,6},{6,7},{7,0},{8,9},{9,10},{10,1... | collective-permute-start | bytes 1179656 | tf_op jit(solution)/shard_map/while/body/eval_jaxpr/ppermute | solution.py:15
  349.6 19.3 %collective-permute-start.1 = (bf16[256,12,64]{0,2,1:T(8,128)(2,1)}, bf16[256,12,64]{0,2,1:T(8,128)(2,1)}, u32[]{:S(2)}, u32[]{:S(2)}) collective-permute-start(bf16[256,12,64]{0,2,1:T(8,128)(2,1)} %copy.77), channel_id=1, source_target_pairs={{0,1},{1,2},{2,3},{3,4},{4,5},{5,6},{6,7},{7,0},{8,9},{9,10},{10,1... | collective-permute-start | bytes 1179656 | tf_op jit(solution)/shard_map/while/body/eval_jaxpr/ppermute | solution.py:15
  377.6 9.3 %collective-permute-start.2 = (bf16[256,12,64]{0,2,1:T(8,128)(2,1)}, bf16[256,12,64]{0,2,1:T(8,128)(2,1)}, u32[]{:S(2)}, u32[]{:S(2)}) collective-permute-start(bf16[256,12,64]{0,2,1:T(8,128)(2,1)} %fusion.189), channel_id=1, source_target_pairs={{0,1},{1,2},{2,3},{3,4},{4,5},{5,6},{6,7},{7,0},{8,9},{9,10},{10,1... | collective-permute-start | bytes 1179656 | tf_op jit(solution)/shard_map/while/body/eval_jaxpr/ppermute | solution.py:15
  380.3 10.9 %collective-permute-start.3 = (bf16[256,12,64]{0,2,1:T(8,128)(2,1)}, bf16[256,12,64]{0,2,1:T(8,128)(2,1)}, u32[]{:S(2)}, u32[]{:S(2)}) collective-permute-start(bf16[256,12,64]{0,2,1:T(8,128)(2,1)} %fusion.190), channel_id=1, source_target_pairs={{0,1},{1,2},{2,3},{3,4},{4,5},{5,6},{6,7},{7,0},{8,9},{9,10},{10,1... | collective-permute-start | bytes 1179656 | tf_op jit(solution)/shard_map/while/body/eval_jaxpr/ppermute | solution.py:15
  380.3 15.1 %collective-permute-start = (bf16[256,12,64]{0,2,1:T(8,128)(2,1)S(1)}, bf16[256,12,64]{0,2,1:T(8,128)(2,1)}, u32[]{:S(2)}, u32[]{:S(2)}) collective-permute-start(bf16[256,12,64]{0,2,1:T(8,128)(2,1)S(1)} %copy.76), channel_id=1, source_target_pairs={{0,1},{1,2},{2,3},{3,4},{4,5},{5,6},{6,7},{7,0},{8,9},{9,10},{10,1... | collective-permute-start | bytes 1179656 | tf_op jit(solution)/shard_map/while/body/eval_jaxpr/ppermute | solution.py:15
  380.3 19.3 %collective-permute-start.1 = (bf16[256,12,64]{0,2,1:T(8,128)(2,1)}, bf16[256,12,64]{0,2,1:T(8,128)(2,1)}, u32[]{:S(2)}, u32[]{:S(2)}) collective-permute-start(bf16[256,12,64]{0,2,1:T(8,128)(2,1)} %copy.77), channel_id=1, source_target_pairs={{0,1},{1,2},{2,3},{3,4},{4,5},{5,6},{6,7},{7,0},{8,9},{9,10},{10,1... | collective-permute-start | bytes 1179656 | tf_op jit(solution)/shard_map/while/body/eval_jaxpr/ppermute | solution.py:15
  408.2 9.3 %collective-permute-start.2 = (bf16[256,12,64]{0,2,1:T(8,128)(2,1)}, bf16[256,12,64]{0,2,1:T(8,128)(2,1)}, u32[]{:S(2)}, u32[]{:S(2)}) collective-permute-start(bf16[256,12,64]{0,2,1:T(8,128)(2,1)} %fusion.189), channel_id=1, source_target_pairs={{0,1},{1,2},{2,3},{3,4},{4,5},{5,6},{6,7},{7,0},{8,9},{9,10},{10,1... | collective-permute-start | bytes 1179656 | tf_op jit(solution)/shard_map/while/body/eval_jaxpr/ppermute | solution.py:15
  410.9 10.8 %collective-permute-start.3 = (bf16[256,12,64]{0,2,1:T(8,128)(2,1)}, bf16[256,12,64]{0,2,1:T(8,128)(2,1)}, u32[]{:S(2)}, u32[]{:S(2)}) collective-permute-start(bf16[256,12,64]{0,2,1:T(8,128)(2,1)} %fusion.190), channel_id=1, source_target_pairs={{0,1},{1,2},{2,3},{3,4},{4,5},{5,6},{6,7},{7,0},{8,9},{9,10},{10,1... | collective-permute-start | bytes 1179656 | tf_op jit(solution)/shard_map/while/body/eval_jaxpr/ppermute | solution.py:15
  410.9 15.0 %collective-permute-start = (bf16[256,12,64]{0,2,1:T(8,128)(2,1)S(1)}, bf16[256,12,64]{0,2,1:T(8,128)(2,1)}, u32[]{:S(2)}, u32[]{:S(2)}) collective-permute-start(bf16[256,12,64]{0,2,1:T(8,128)(2,1)S(1)} %copy.76), channel_id=1, source_target_pairs={{0,1},{1,2},{2,3},{3,4},{4,5},{5,6},{6,7},{7,0},{8,9},{9,10},{10,1... | collective-permute-start | bytes 1179656 | tf_op jit(solution)/shard_map/while/body/eval_jaxpr/ppermute | solution.py:15
  410.9 19.2 %collective-permute-start.1 = (bf16[256,12,64]{0,2,1:T(8,128)(2,1)}, bf16[256,12,64]{0,2,1:T(8,128)(2,1)}, u32[]{:S(2)}, u32[]{:S(2)}) collective-permute-start(bf16[256,12,64]{0,2,1:T(8,128)(2,1)} %copy.77), channel_id=1, source_target_pairs={{0,1},{1,2},{2,3},{3,4},{4,5},{5,6},{6,7},{7,0},{8,9},{9,10},{10,1... | collective-permute-start | bytes 1179656 | tf_op jit(solution)/shard_map/while/body/eval_jaxpr/ppermute | solution.py:15
  438.8 9.3 %collective-permute-start.2 = (bf16[256,12,64]{0,2,1:T(8,128)(2,1)}, bf16[256,12,64]{0,2,1:T(8,128)(2,1)}, u32[]{:S(2)}, u32[]{:S(2)}) collective-permute-start(bf16[256,12,64]{0,2,1:T(8,128)(2,1)} %fusion.189), channel_id=1, source_target_pairs={{0,1},{1,2},{2,3},{3,4},{4,5},{5,6},{6,7},{7,0},{8,9},{9,10},{10,1... | collective-permute-start | bytes 1179656 | tf_op jit(solution)/shard_map/while/body/eval_jaxpr/ppermute | solution.py:15
  441.5 10.9 %collective-permute-start.3 = (bf16[256,12,64]{0,2,1:T(8,128)(2,1)}, bf16[256,12,64]{0,2,1:T(8,128)(2,1)}, u32[]{:S(2)}, u32[]{:S(2)}) collective-permute-start(bf16[256,12,64]{0,2,1:T(8,128)(2,1)} %fusion.190), channel_id=1, source_target_pairs={{0,1},{1,2},{2,3},{3,4},{4,5},{5,6},{6,7},{7,0},{8,9},{9,10},{10,1... | collective-permute-start | bytes 1179656 | tf_op jit(solution)/shard_map/while/body/eval_jaxpr/ppermute | solution.py:15
  441.5 15.1 %collective-permute-start = (bf16[256,12,64]{0,2,1:T(8,128)(2,1)S(1)}, bf16[256,12,64]{0,2,1:T(8,128)(2,1)}, u32[]{:S(2)}, u32[]{:S(2)}) collective-permute-start(bf16[256,12,64]{0,2,1:T(8,128)(2,1)S(1)} %copy.76), channel_id=1, source_target_pairs={{0,1},{1,2},{2,3},{3,4},{4,5},{5,6},{6,7},{7,0},{8,9},{9,10},{10,1... | collective-permute-start | bytes 1179656 | tf_op jit(solution)/shard_map/while/body/eval_jaxpr/ppermute | solution.py:15
  441.5 19.3 %collective-permute-start.1 = (bf16[256,12,64]{0,2,1:T(8,128)(2,1)}, bf16[256,12,64]{0,2,1:T(8,128)(2,1)}, u32[]{:S(2)}, u32[]{:S(2)}) collective-permute-start(bf16[256,12,64]{0,2,1:T(8,128)(2,1)} %copy.77), channel_id=1, source_target_pairs={{0,1},{1,2},{2,3},{3,4},{4,5},{5,6},{6,7},{7,0},{8,9},{9,10},{10,1... | collective-permute-start | bytes 1179656 | tf_op jit(solution)/shard_map/while/body/eval_jaxpr/ppermute | solution.py:15
  469.4 9.3 %collective-permute-start.2 = (bf16[256,12,64]{0,2,1:T(8,128)(2,1)}, bf16[256,12,64]{0,2,1:T(8,128)(2,1)}, u32[]{:S(2)}, u32[]{:S(2)}) collective-permute-start(bf16[256,12,64]{0,2,1:T(8,128)(2,1)} %fusion.189), channel_id=1, source_target_pairs={{0,1},{1,2},{2,3},{3,4},{4,5},{5,6},{6,7},{7,0},{8,9},{9,10},{10,1... | collective-permute-start | bytes 1179656 | tf_op jit(solution)/shard_map/while/body/eval_jaxpr/ppermute | solution.py:15
  472.0 10.9 %collective-permute-start.3 = (bf16[256,12,64]{0,2,1:T(8,128)(2,1)}, bf16[256,12,64]{0,2,1:T(8,128)(2,1)}, u32[]{:S(2)}, u32[]{:S(2)}) collective-permute-start(bf16[256,12,64]{0,2,1:T(8,128)(2,1)} %fusion.190), channel_id=1, source_target_pairs={{0,1},{1,2},{2,3},{3,4},{4,5},{5,6},{6,7},{7,0},{8,9},{9,10},{10,1... | collective-permute-start | bytes 1179656 | tf_op jit(solution)/shard_map/while/body/eval_jaxpr/ppermute | solution.py:15
  472.0 15.1 %collective-permute-start = (bf16[256,12,64]{0,2,1:T(8,128)(2,1)S(1)}, bf16[256,12,64]{0,2,1:T(8,128)(2,1)}, u32[]{:S(2)}, u32[]{:S(2)}) collective-permute-start(bf16[256,12,64]{0,2,1:T(8,128)(2,1)S(1)} %copy.76), channel_id=1, source_target_pairs={{0,1},{1,2},{2,3},{3,4},{4,5},{5,6},{6,7},{7,0},{8,9},{9,10},{10,1... | collective-permute-start | bytes 1179656 | tf_op jit(solution)/shard_map/while/body/eval_jaxpr/ppermute | solution.py:15
  472.0 19.3 %collective-permute-start.1 = (bf16[256,12,64]{0,2,1:T(8,128)(2,1)}, bf16[256,12,64]{0,2,1:T(8,128)(2,1)}, u32[]{:S(2)}, u32[]{:S(2)}) collective-permute-start(bf16[256,12,64]{0,2,1:T(8,128)(2,1)} %copy.77), channel_id=1, source_target_pairs={{0,1},{1,2},{2,3},{3,4},{4,5},{5,6},{6,7},{7,0},{8,9},{9,10},{10,1... | collective-permute-start | bytes 1179656 | tf_op jit(solution)/shard_map/while/body/eval_jaxpr/ppermute | solution.py:15
  499.9 9.3 %collective-permute-start.2 = (bf16[256,12,64]{0,2,1:T(8,128)(2,1)}, bf16[256,12,64]{0,2,1:T(8,128)(2,1)}, u32[]{:S(2)}, u32[]{:S(2)}) collective-permute-start(bf16[256,12,64]{0,2,1:T(8,128)(2,1)} %fusion.189), channel_id=1, source_target_pairs={{0,1},{1,2},{2,3},{3,4},{4,5},{5,6},{6,7},{7,0},{8,9},{9,10},{10,1... | collective-permute-start | bytes 1179656 | tf_op jit(solution)/shard_map/while/body/eval_jaxpr/ppermute | solution.py:15
  502.6 10.9 %collective-permute-start.3 = (bf16[256,12,64]{0,2,1:T(8,128)(2,1)}, bf16[256,12,64]{0,2,1:T(8,128)(2,1)}, u32[]{:S(2)}, u32[]{:S(2)}) collective-permute-start(bf16[256,12,64]{0,2,1:T(8,128)(2,1)} %fusion.190), channel_id=1, source_target_pairs={{0,1},{1,2},{2,3},{3,4},{4,5},{5,6},{6,7},{7,0},{8,9},{9,10},{10,1... | collective-permute-start | bytes 1179656 | tf_op jit(solution)/shard_map/while/body/eval_jaxpr/ppermute | solution.py:15
  502.6 15.1 %collective-permute-start = (bf16[256,12,64]{0,2,1:T(8,128)(2,1)S(1)}, bf16[256,12,64]{0,2,1:T(8,128)(2,1)}, u32[]{:S(2)}, u32[]{:S(2)}) collective-permute-start(bf16[256,12,64]{0,2,1:T(8,128)(2,1)S(1)} %copy.76), channel_id=1, source_target_pairs={{0,1},{1,2},{2,3},{3,4},{4,5},{5,6},{6,7},{7,0},{8,9},{9,10},{10,1... | collective-permute-start | bytes 1179656 | tf_op jit(solution)/shard_map/while/body/eval_jaxpr/ppermute | solution.py:15
  502.6 19.3 %collective-permute-start.1 = (bf16[256,12,64]{0,2,1:T(8,128)(2,1)}, bf16[256,12,64]{0,2,1:T(8,128)(2,1)}, u32[]{:S(2)}, u32[]{:S(2)}) collective-permute-start(bf16[256,12,64]{0,2,1:T(8,128)(2,1)} %copy.77), channel_id=1, source_target_pairs={{0,1},{1,2},{2,3},{3,4},{4,5},{5,6},{6,7},{7,0},{8,9},{9,10},{10,1... | collective-permute-start | bytes 1179656 | tf_op jit(solution)/shard_map/while/body/eval_jaxpr/ppermute | solution.py:15
  530.5 9.3 %collective-permute-start.2 = (bf16[256,12,64]{0,2,1:T(8,128)(2,1)}, bf16[256,12,64]{0,2,1:T(8,128)(2,1)}, u32[]{:S(2)}, u32[]{:S(2)}) collective-permute-start(bf16[256,12,64]{0,2,1:T(8,128)(2,1)} %fusion.189), channel_id=1, source_target_pairs={{0,1},{1,2},{2,3},{3,4},{4,5},{5,6},{6,7},{7,0},{8,9},{9,10},{10,1... | collective-permute-start | bytes 1179656 | tf_op jit(solution)/shard_map/while/body/eval_jaxpr/ppermute | solution.py:15
  533.1 10.9 %collective-permute-start.3 = (bf16[256,12,64]{0,2,1:T(8,128)(2,1)}, bf16[256,12,64]{0,2,1:T(8,128)(2,1)}, u32[]{:S(2)}, u32[]{:S(2)}) collective-permute-start(bf16[256,12,64]{0,2,1:T(8,128)(2,1)} %fusion.190), channel_id=1, source_target_pairs={{0,1},{1,2},{2,3},{3,4},{4,5},{5,6},{6,7},{7,0},{8,9},{9,10},{10,1... | collective-permute-start | bytes 1179656 | tf_op jit(solution)/shard_map/while/body/eval_jaxpr/ppermute | solution.py:15
  533.1 15.1 %collective-permute-start = (bf16[256,12,64]{0,2,1:T(8,128)(2,1)S(1)}, bf16[256,12,64]{0,2,1:T(8,128)(2,1)}, u32[]{:S(2)}, u32[]{:S(2)}) collective-permute-start(bf16[256,12,64]{0,2,1:T(8,128)(2,1)S(1)} %copy.76), channel_id=1, source_target_pairs={{0,1},{1,2},{2,3},{3,4},{4,5},{5,6},{6,7},{7,0},{8,9},{9,10},{10,1... | collective-permute-start | bytes 1179656 | tf_op jit(solution)/shard_map/while/body/eval_jaxpr/ppermute | solution.py:15
  533.1 19.3 %collective-permute-start.1 = (bf16[256,12,64]{0,2,1:T(8,128)(2,1)}, bf16[256,12,64]{0,2,1:T(8,128)(2,1)}, u32[]{:S(2)}, u32[]{:S(2)}) collective-permute-start(bf16[256,12,64]{0,2,1:T(8,128)(2,1)} %copy.77), channel_id=1, source_target_pairs={{0,1},{1,2},{2,3},{3,4},{4,5},{5,6},{6,7},{7,0},{8,9},{9,10},{10,1... | collective-permute-start | bytes 1179656 | tf_op jit(solution)/shard_map/while/body/eval_jaxpr/ppermute | solution.py:15
  559.5 133.5 %all-reduce.20.cloned.1.call-start = ((), (), s32[]{:S(2)}) async-start(), calls=%async_computation.14 | async-start | bytes 7077888 | tf_op jit(solution)/shard_map/psum | solution.py:292
  563.0 4.8 copy-start.44
  569.9 36.5 %copy-start.42 = (bf16[3072]{0:T(1024)(128)(2,1)S(1)}, bf16[3072]{0:T(1024)(128)(2,1)}, u32[]{:S(2)}) copy-start(bf16[3072]{0:T(1024)(128)(2,1)} %get-tuple-element.586) | copy-start | bytes 18436
  569.9 71.1 %copy-start.11 = (bf16[256,3072]{1,0:T(8,128)(2,1)S(1)}, bf16[256,3072]{1,0:T(8,128)(2,1)}, u32[]{:S(2)}) copy-start(bf16[256,3072]{1,0:T(8,128)(2,1)} %copy-done.10) | copy-start | bytes 4718596
  638.8 61.1 %copy-start.43 = (f32[192]{0:T(256)}, f32[192]{0:T(256)S(1)}, u32[]{:S(2)}) copy-start(f32[192]{0:T(256)S(1)} %convert_element_type.269) | copy-start | bytes 2308
  (64 other events, 133.2 us)
Sparse Core Ops, SparseCore 0:
  9.9 50.0 all-gather.9
  68.5 39.1 all-gather.11
  109.9 39.1 all-gather.19
  150.8 55.2 all-gather.15
  207.8 57.0 all-gather.17
  266.6 27.7 all-gather.13
  297.3 28.5 reduce-scatter.6
  328.8 57.0 reduce-scatter.8
  388.9 57.0 reduce-scatter.10
  559.6 44.8 reduce-scatter.4
  607.1 85.8 all-reduce.19
where the time goes:
time: 711 us; the launch traced here: 707 us
  waiting for transfers between devices  329 us (46%)
  matrix products  151 us (21%)
  blocking collectives  69.9 us (10%)
  other arithmetic  63.4 us (9%)
  local copies, waits for them, and re-layouts  62.1 us (9%)
  between operations  17.8 us (3%)
  loops' own time  8.68 us (1%)
    ppermute x32, waiting for transfers between devices, from_behind(): return lax.ppermute(x, axis, [(i, (i + by) % size) for i in range(size)])  113 us
    psum x1, waiting for transfers between devices, on_device(): lax.psum(shares[0].astype(jnp.bfloat16), 'ctx').astype(jnp.float32)  45.3 us
    all_gather x1, waiting for transfers between devices, on_device(): value_piece = lax.all_gather(values, 'ctx', axis=0, tiled=True)  41.4 us
    all_gather x1, waiting for transfers between devices, on_device(): lax.all_gather(down_weight, 'fsdp', axis=0, tiled=True)  38.2 us
    reduce_scatter x1, waiting for transfers between devices, on_device(): lax.psum_scatter(in_weight_part.astype(jnp.bfloat16), 'fsdp', scatter_dim...  34.4 us
    unnamed x2, blocking collectives  33.7 us
    while x108, local copies, waits for them, and re-layouts  31 us
    all_gather x1, waiting for transfers between devices, on_device(): lax.all_gather(in_weight, 'fsdp', axis=0, tiled=True)  22.8 us
  transfers between devices with their start and end apart: 43, of which 39 were waited for; matrix products, arithmetic and copies ran while one was open for 35% of the time, Pallas kernels for 0%

commit v1 on v0

--- a/solution.py
+++ b/solution.py
@@ -3,6 +3,7 @@
 import jax.numpy as jnp
 from jax import lax
 from jax.sharding import PartitionSpec as P
+from jax.lax import axis_index, axis_size, ppermute
 
 HEAD = 64
 ROT = 16
@@ -169,7 +170,26 @@
     )
     carry = start_state
     key_piece = lax.all_gather(keys, "ctx", axis=0, tiled=True)
-    value_piece = lax.all_gather(values, "ctx", axis=0, tiled=True)
+    state_next, block_next, piece_now = (axis_size("ctx"), axis_index("ctx"), values.shape[0])
+    ledger = [b * state_next if jj == 0 else b for jj, b in enumerate(values.shape)]
+    value_piece = lax.dynamic_update_slice_in_dim(
+        jnp.zeros(ledger, values.dtype), values, block_next * piece_now, axis=0
+    )
+    arr_out = then = values
+    num = 1
+    while num < state_next // 2 + 1:
+        arr_out = ppermute(
+            arr_out, "ctx", [(jj, (jj + 1) % state_next) for jj in range(state_next)]
+        )
+        value_piece = lax.dynamic_update_slice_in_dim(
+            value_piece, arr_out, (block_next - num) % state_next * piece_now, axis=0
+        )
+        if 2 * num < state_next:
+            then = ppermute(then, "ctx", [(jj, (jj - 1) % state_next) for jj in range(state_next)])
+            value_piece = lax.dynamic_update_slice_in_dim(
+                value_piece, then, (block_next + num) % state_next * piece_now, axis=0
+            )
+        num += 1
     count = key_piece.shape[0]
     size = 512
 

time: 711 us -> 686 us (0.965)
  waiting for transfers between devices: 329 us -> 271 us
  blocking collectives: 69.9 us -> 79.9 us
  starting transfers between devices: 5.51 us -> 15.3 us
  local copies, waits for them, and re-layouts: 62.1 us -> 70.7 us
    all_gather x1 -> x0, waiting for transfers between devices: 41.4 us -> none  [on_device(): value_piece = lax.all_gather(values, 'ctx', axis=0, tiled=True)]
    all_gather x1, waiting for transfers between devices: 38.2 us -> 7.83 us  [on_device(): lax.all_gather(down_weight, 'fsdp', axis=0, tiled=True)]
    ppermute x0 -> x7, waiting for transfers between devices: none -> 28.2 us  [the longest x4 20.7 us: on_device(): ppermute(arr_out, 'ctx', [(jj, (jj + 1) % state_next) for jj in range(sta...]
    all_gather x1, waiting for transfers between devices: 13.7 us -> 0.01 us  [on_device(): key_piece = lax.all_gather(keys, 'ctx', axis=0, tiled=True)]
    ppermute x0 -> x7, starting transfers between devices: none -> 10.1 us  [the longest x3 9.6 us: on_device(): ppermute(then, 'ctx', [(jj, (jj - 1) % state_next) for jj in range(state_...]
    dynamic_update_slice x0 -> x8, local copies, waits for them, and re-layouts: none -> 9.79 us  [the longest x4 5.38 us: on_device(): lax.dynamic_update_slice_in_dim(value_piece, arr_out, (block_next - num)...]
    all_gather x1, blocking collectives: 12.8 us -> 22.5 us  [on_device(): all_pos = lax.all_gather(query_pos, 'ctx', axis=0, tiled=True)]
  transfers between devices with their start and end apart: 43 -> 49, of which waited for: 39 -> 42; matrix products, arithmetic and copies ran while one was open for 35% -> 38% of each run, Pallas kernels for 0% -> 0%
where the time goes in v1:
time: 686 us; the launch traced here: 682 us
  waiting for transfers between devices  271 us (40%)
  matrix products  151 us (22%)
  blocking collectives  79.9 us (12%)
  local copies, waits for them, and re-layouts  70.7 us (10%)
  other arithmetic  67.3 us (10%)
  between operations  18.1 us (3%)
  starting transfers between devices  15.3 us (2%)
  loops' own time  8.69 us (1%)
    ppermute x32, waiting for transfers between devices, from_behind(): return lax.ppermute(x, axis, [(i, (i + by) % size) for i in range(size)])  113 us
    psum x1, waiting for transfers between devices, on_device(): lax.psum(shares[0].astype(jnp.bfloat16), 'ctx').astype(jnp.float32)  45.1 us
    reduce_scatter x1, waiting for transfers between devices, on_device(): lax.psum_scatter(in_weight_part.astype(jnp.bfloat16), 'fsdp', scatter_dim...  34.3 us
    unnamed x2, blocking collectives  33.7 us
    while x108, local copies, waits for them, and re-layouts  30.4 us
    all_gather x1, waiting for transfers between devices, on_device(): lax.all_gather(in_weight, 'fsdp', axis=0, tiled=True)  22.8 us
    all_gather x1, blocking collectives, on_device(): all_pos = lax.all_gather(query_pos, 'ctx', axis=0, tiled=True)  22.5 us
    dot_general x4, matrix products, softmax_step(): jnp.einsum('qhd,khd->hqk', queries, keys, preferred_element_type=jnp.floa...  22.1 us
  transfers between devices with their start and end apart: 49, of which 42 were waited for; matrix products, arithmetic and copies ran while one was open for 38% of the time, Pallas kernels for 0%

profile of v1, /device:TPU:0, one launch (start us, length us, event | category | flops | bytes accessed | tf_op | source)
XLA Modules:
  0.0 682.0 jit_solution(3325261085705835145)
XLA Ops:
  14.8 18.4 %all-reduce.17 = (bf16[768]{0:T(1024)(128)(2,1)}, bf16[768]{0:T(1024)(128)(2,1)}, bf16[2304]{0:T(1024)(128)(2,1)S(1)}, bf16[768]{0:T(1024)(128)(2,1)S(1)}, bf16[768]{0:T(1024)(128)(2,1)S(1)}) all-reduce(bf16[768]{0:T(1024)(128)(2,1)S(1)} %dynamic-update-slice.5, ...), channel_id=1, replica_groups=mesh['fsdp'=4,'ctx'=8] {'fsdp'}, use_global_device_ids=true, to_apply=%add.5 | all-reduce | flops 5376 | bytes 21504
  37.1 22.8 %all-gather.8.cloned.1.call-done = bf16[768,2304]{1,0:T(8,128)(2,1)} async-done(((bf16[192,2304]{1,0:T(8,128)(2,1)}), bf16[768,2304]{1,0:T(8,128)(2,1)}) %all-gather.8.cloned.1.call-update) | async-done | bytes 3538960 | tf_op jit(solution)/shard_map/all_gather | solution.py:110
  60.0 4.7 convolution_add_fusion
  73.3 3.5 collective-permute-start.5
  76.8 11.5 %collective-permute-done.4 = bf16[256,12,64]{0,2,1:T(8,128)(2,1)S(1)} collective-permute-done((bf16[256,12,64]{0,2,1:T(8,128)(2,1)}, bf16[256,12,64]{0,2,1:T(8,128)(2,1)S(1)}, u32[]{:S(2)}, u32[]{:S(2)}) %collective-permute-start.4) | collective-permute-done | bytes 393248 | tf_op jit(solution)/shard_map/ppermute | solution.py:181
  88.4 5.0 collective-permute-done.5
  93.4 3.7 collective-permute-start.7
  97.2 6.7 collective-permute-done.6
  108.1 8.3 %all-gather.1 = bf16[4,1,768]{2,1,0:T(2,128)(2,1)S(1)} all-gather(bf16[1,1,768]{2,1,0:T(2,128)(2,1)S(1)} %reshape.292), channel_id=1, replica_groups=mesh['fsdp'=4,'ctx'=8] {'fsdp'}, dimensions={0}, use_global_device_ids=true | all-gather | bytes 7680 | tf_op jit(solution)/shard_map/all_gather | solution.py:115
  117.0 22.5 %all-gather = s32[1,2048]{1,0:T(1,128)} all-gather(s32[1,256]{1,0:T(1,128)} %param.20), channel_id=2, replica_groups=mesh['fsdp'=4,'ctx'=8] {'ctx'}, dimensions={1}, use_global_device_ids=true | all-gather | bytes 9216 | tf_op jit(solution)/shard_map/all_gather | solution.py:142
  156.7 63.9 %while.39 = (s32[]{:T(128)}, f32[12,256]{1,0:T(8,128)S(1)}, f32[12,256]{1,0:T(8,128)S(1)}, f32[256,12,64]{0,2,1:T(8,128)S(1)}, s32[4]{0:T(128)S(1)}, /*index=5*/...) while((s32[]{:T(128)}, f32[12,256]{1,0:T(8,128)S(1)}, ...), condition=%wide.region_5.6_spmd.clone, body=%wide.region_2.5_spmd.clone.sunk | while | flops 420694016 | bytes 48307420 | solution.py:203
  160.9 5.5 fusion.175
  166.4 4.8 fusion.179
  176.7 5.5 fusion.175
  182.3 4.8 fusion.179
  192.6 5.6 fusion.175
  198.2 4.8 fusion.179
  208.5 5.4 fusion.175
  214.0 5.2 fusion.179
  222.7 11.4 %multiply_convert_fusion.1 = (bf16[256,3072]{1,0:T(8,128)(2,1)S(1)}, f32[256,3072]{1,0:T(8,128)}, f32[256,3072]{1,0:T(8,128)}) fusion(f32[3072]{0:T(1024)S(1)} %bitcast.231, bf16[768,3072]{1,0:T(8,128)(2,1)} %all-gather.14.cloned.1.call-done, bf16[1,256,768]{2,1,0:T(8,128)(2,1)S(1)} %copy-done.3, f32[768]{0:T(1024)S(1)} %copy-done.32, ...), kind=kOutput, calls=%fused_computation.54 | convolution fusion | flops 1261043712 | bytes 12996608 | tf_op jit(solution)/shard_map/dot_general | solution.py:208
  234.1 7.8 %all-gather.16.cloned.1.call-done = bf16[3072,768]{1,0:T(8,128)(2,1)} async-done(((bf16[768,768]{1,0:T(8,128)(2,1)}), bf16[3072,768]{1,0:T(8,128)(2,1)}) %all-gather.16.cloned.1.call-update) | async-done | bytes 4718608 | tf_op jit(solution)/shard_map/all_gather | solution.py:116
  242.0 6.8 %fusion.121 = (bf16[3072]{0:T(1024)(128)(2,1)}, bf16[256,3072]{1,0:T(8,128)(2,1)S(1)}) fusion(f32[256,3072]{1,0:T(8,128)} %get-tuple-element.563, f32[256,3072]{1,0:T(8,128)} %get-tuple-element.587, bf16[3072,768]{1,0:T(8,128)(2,1)} %all-gather.16.cloned.1.call-done, bf16[1,256,768]{2,1,0:T(8,128)(2,1)S(1)} %copy-done.4), kind=kOutput, calls=%fused_computation.181 | convolution fusion | flops 1219752960 | bytes 12982272 | tf_op jit(solution)/shard_map/dot_general | solution.py:48
  249.9 3.7 convolution_convert_fusion.1
  253.8 17.6 %all-gather.12.cloned.1.call-done = bf16[768,768]{1,0:T(8,128)(2,1)} async-done(((bf16[192,768]{1,0:T(8,128)(2,1)}), bf16[768,768]{1,0:T(8,128)(2,1)}) %all-gather.12.cloned.1.call-update) | async-done | bytes 1179664 | tf_op jit(solution)/shard_map/all_gather | solution.py:112
  275.8 3.5 convolution_convert_fusion
  283.0 244.8 %while.40 = (s32[]{:T(128)}, bf16[256,12,64]{0,2,1:T(8,128)(2,1)}, bf16[256,12,64]{0,2,1:T(8,128)(2,1)}, f32[256,12,64]{0,2,1:T(8,128)S(1)}, f32[256,12,64]{0,2,...) while((s32[]{:T(128)}, bf16[256,12,64]{0,2,1:T(8,128)(2,1)}, ...), condition=%wide.region_9.10_spmd.clone, body=%wide.region_8.9_spmd.clone.sunk | while | flops 513605632 | bytes 40837772 | solution.py:260
  291.6 2.6 fusion.192
  302.0 3.1 collective-permute-done.3
  309.3 4.2 collective-permute-done.1
  322.2 2.7 fusion.192
  327.8 3.6 collective-permute-done.2
  332.6 3.1 collective-permute-done.3
  339.9 4.2 collective-permute-done.1
  352.8 2.6 fusion.192
  357.0 5.1 collective-permute-done.2
  363.1 3.1 collective-permute-done.3
  370.5 4.2 collective-permute-done.1
  387.7 5.0 collective-permute-done.2
  393.8 3.1 collective-permute-done.3
  401.2 4.2 collective-permute-done.1
  414.1 2.6 fusion.192
  418.4 5.1 collective-permute-done.2
  424.5 3.1 collective-permute-done.3
  431.8 4.2 collective-permute-done.1
  444.7 2.6 fusion.192
  448.9 5.1 collective-permute-done.2
  455.1 3.1 collective-permute-done.3
  462.4 4.2 collective-permute-done.1
  475.3 2.6 fusion.192
  479.5 5.1 collective-permute-done.2
  485.6 3.1 collective-permute-done.3
  493.0 4.2 collective-permute-done.1
  505.8 2.6 fusion.192
  510.1 5.1 collective-permute-done.2
  516.2 3.1 collective-permute-done.3
  523.6 4.2 collective-permute-done.1
  531.6 3.2 convolution_convert_fusion.2
  538.3 4.5 fusion.123
  545.1 34.3 %reduce-scatter.5.cloned.1.call-done = bf16[192,2304]{1,0:T(8,128)(2,1)} async-done(((bf16[768,2304]{1,0:T(8,128)(2,1)}), bf16[192,2304]{1,0:T(8,128)(2,1)}) %reduce-scatter.5.cloned.1.call-update) | async-done | bytes 884752 | tf_op jit(solution)/shard_map/reduce_scatter | solution.py:277
  581.3 15.4 %all-reduce.16 = (bf16[768]{0:T(1024)(128)(2,1)S(1)}, bf16[768]{0:T(1024)(128)(2,1)S(1)}, bf16[2304]{0:T(1024)(128)(2,1)S(1)}, bf16[768]{0:T(1024)(128)(2,1)S(1)...) all-reduce(bf16[768]{0:T(1024)(128)(2,1)S(1)} %dynamic-update-slice, ...), channel_id=1, replica_groups=mesh['fsdp'=4,'ctx'=8] {'fsdp'}, use_global_device_ids=true, to_apply=%add.6 | all-reduce | flops 10752 | bytes 43008
  597.2 15.3 %all-reduce.14 = (bf16[576]{0:T(1024)(128)(2,1)S(1)}, bf16[192]{0:T(256)(128)(2,1)S(1)}, bf16[768]{0:T(1024)(128)(2,1)S(1)}, bf16[192]{0:T(256)(128)(2,1)S(1)}, ...) all-reduce(bf16[576]{0:T(1024)(128)(2,1)S(1)} %dynamic-slice.8, ...), channel_id=1, replica_groups=mesh['fsdp'=4,'ctx'=8] {'ctx'}, use_global_device_ids=true, to_apply=%region_16.17 | all-reduce | flops 2304 | bytes 9216 | tf_op jit(solution)/shard_map/psum | solution.py:313
  616.0 3.9 convolution_add_fusion.3
  622.6 45.1 %all-reduce.20.cloned.1.call-done = (bf16[192,2304]{1,0:T(8,128)(2,1)}, bf16[192,768]{1,0:T(8,128)(2,1)}, bf16[192,3072]{1,0:T(8,128)(2,1)}, bf16[768,768]{1,0:T(8,128)(2,1)}) async-done(((bf16[192,2304]{1,0:T(8,128)(2,1)}, bf16[192,768]{1,0:T(8,128)(2,1)}, bf16[192,3072]{1,0:T(8,128)(2,1)}, bf16[768,768]{1,0:T(8,128)(2,1)}), (bf16[192,2304]{1,0:T(8,128)(2,1)}, bf16[192,768]{1,0:T(8,128)(2,1)}, ...) | async-done | bytes 3538960 | tf_op jit(solution)/shard_map/psum | solution.py:312
  667.7 3.1 convert_element_type.271
  (460 shorter events, 219.2 us)
Async XLA Ops:
  7.2 52.8 %all-gather.8.cloned.1.call-start = ((), (), s32[]{:S(2)}) async-start(), calls=%async_computation.4 | async-start | bytes 4423680 | tf_op jit(solution)/shard_map/all_gather | solution.py:110
  7.9 148.8 %all-gather.10.cloned.1.call-start = ((), (), s32[]{:S(2)}) async-start(), calls=%async_computation.5 | async-start | bytes 3538944 | tf_op jit(solution)/shard_map/all_gather | solution.py:172
  33.2 26.7 %copy-start.24 = (f32[768]{0:T(1024)}, f32[768]{0:T(1024)S(1)}, u32[]{:S(2)}) copy-start(f32[768]{0:T(1024)S(1)} %convert_element_type.241) | copy-start | bytes 9220
  33.2 26.7 %copy-start.30 = (f32[768]{0:T(1024)}, f32[768]{0:T(1024)S(1)}, u32[]{:S(2)}) copy-start(f32[768]{0:T(1024)S(1)} %convert_element_type.242) | copy-start | bytes 9220
  34.7 32.3 %copy-start.28 = (f32[256,16]{0,1:T(8,128)}, f32[256,16]{0,1:T(8,128)S(1)}, u32[]{:S(2)}) copy-start(f32[256,16]{0,1:T(8,128)S(1)} %get-tuple-element.584) | copy-start | bytes 49156
  35.8 24.1 %copy-start.34 = (f32[256]{0:T(256)}, f32[256]{0:T(256)S(1)}, u32[]{:S(2)}) copy-start(f32[256]{0:T(256)S(1)} %broadcast_multiply_fusion.1) | copy-start | bytes 3076
  37.1 22.9 %copy-start.43 = (f32[256]{0:T(256)}, f32[256]{0:T(256)S(1)}, u32[]{:S(2)}) copy-start(f32[256]{0:T(256)S(1)} %fusion.73) | copy-start | bytes 3076
  37.1 22.9 %copy-start.37 = (f32[256]{0:T(256)}, f32[256]{0:T(256)S(1)}, u32[]{:S(2)}) copy-start(f32[256]{0:T(256)S(1)} %fusion.109) | copy-start | bytes 3076
  69.0 153.7 %all-gather.14.cloned.1.call-start = ((), (), s32[]{:S(2)}) async-start(), calls=%async_computation.7 | async-start | bytes 5898240 | tf_op jit(solution)/shard_map/all_gather | solution.py:114
  69.7 172.3 %all-gather.16.cloned.1.call-start = ((), (), s32[]{:S(2)}) async-start(), calls=%async_computation.8 | async-start | bytes 5898240 | tf_op jit(solution)/shard_map/all_gather | solution.py:116
  70.3 201.1 %all-gather.12.cloned.1.call-start = ((), (), s32[]{:S(2)}) async-start(), calls=%async_computation.6 | async-start | bytes 1474560 | tf_op jit(solution)/shard_map/all_gather | solution.py:112
  73.3 15.1 %collective-permute-start.4 = (bf16[256,12,64]{0,2,1:T(8,128)(2,1)}, bf16[256,12,64]{0,2,1:T(8,128)(2,1)S(1)}, u32[]{:S(2)}, u32[]{:S(2)}) collective-permute-start(bf16[256,12,64]{0,2,1:T(8,128)(2,1)} %get-tuple-element.782), channel_id=1, source_target_pairs={{0,1},{1,2},{2,3},{3,4},{4,5},{5,6},{6,7},{7,0},{8,9},{9,10},{10,1... | collective-permute-start | bytes 1179656 | tf_op jit(solution)/shard_map/ppermute | solution.py:181
  73.3 20.1 %collective-permute-start.5 = (bf16[256,12,64]{0,2,1:T(8,128)(2,1)}, bf16[256,12,64]{0,2,1:T(8,128)(2,1)}, u32[]{:S(2)}, u32[]{:S(2)}) collective-permute-start(bf16[256,12,64]{0,2,1:T(8,128)(2,1)} %get-tuple-element.782), channel_id=1, source_target_pairs={{0,7},{1,0},{2,1},{3,2},{4,3},{5,4},{6,5},{7,6},{8,15},{9,8},{10,9... | collective-permute-start | bytes 1179656 | tf_op jit(solution)/shard_map/ppermute | solution.py:188
  88.4 51.2 %copy-start.22 = (bf16[256,12,64]{0,2,1:T(8,128)(2,1)}, bf16[256,12,64]{0,2,1:T(8,128)(2,1)S(1)}, u32[]{:S(2)}) copy-start(bf16[256,12,64]{0,2,1:T(8,128)(2,1)S(1)} %collective-permute-done.4) | copy-start | bytes 1179652
  88.4 15.5 %collective-permute-start.6 = (bf16[256,12,64]{0,2,1:T(8,128)(2,1)S(1)}, bf16[256,12,64]{0,2,1:T(8,128)(2,1)S(1)}, u32[]{:S(2)}, u32[]{:S(2)}) collective-permute-start(bf16[256,12,64]{0,2,1:T(8,128)(2,1)S(1)} %collective-permute-done.4), channel_id=1, source_target_pairs={{0,1},{1,2},{2,3},{3,4},{4,5},{5,6},{6,7},{7,0},{8,9},{9,10},{10,1... | collective-permute-start | bytes 1179656 | tf_op jit(solution)/shard_map/ppermute | solution.py:181
  93.4 48.9 %collective-permute-start.7 = (bf16[256,12,64]{0,2,1:T(8,128)(2,1)}, bf16[256,12,64]{0,2,1:T(8,128)(2,1)S(1)}, u32[]{:S(2)}, u32[]{:S(2)}) collective-permute-start(bf16[256,12,64]{0,2,1:T(8,128)(2,1)} %collective-permute-done.5), channel_id=1, source_target_pairs={{0,7},{1,0},{2,1},{3,2},{4,3},{5,4},{6,5},{7,6},{8,15},{9,8},{10,9... | collective-permute-start | bytes 1179656 | tf_op jit(solution)/shard_map/ppermute | solution.py:188
  97.1 447.9 %reduce-scatter.7.cloned.1.call-start = ((), (), s32[]{:S(2)}) async-start(), calls=%async_computation.10 | async-start | bytes 1474560 | tf_op jit(solution)/shard_map/reduce_scatter | solution.py:283
  103.9 42.7 %collective-permute-start.8 = (bf16[256,12,64]{0,2,1:T(8,128)(2,1)S(1)}, bf16[256,12,64]{0,2,1:T(8,128)(2,1)}, u32[]{:S(2)}, u32[]{:S(2)}) collective-permute-start(bf16[256,12,64]{0,2,1:T(8,128)(2,1)S(1)} %collective-permute-done.6), channel_id=1, source_target_pairs={{0,1},{1,2},{2,3},{3,4},{4,5},{5,6},{6,7},{7,0},{8,9},{9,10},{10,1... | collective-permute-start | bytes 1179656 | tf_op jit(solution)/shard_map/ppermute | solution.py:181
  139.6 17.2 %copy-start.50 = (s32[4]{0:T(128)S(1)}, s32[4]{0:T(128)}, u32[]{:S(2)}) copy-start(s32[4]{0:T(128)} %iota_multiply_fusion) | copy-start | bytes 52
  142.3 10.3 %collective-permute-start.9 = (bf16[256,12,64]{0,2,1:T(8,128)(2,1)S(1)}, bf16[256,12,64]{0,2,1:T(8,128)(2,1)S(1)}, u32[]{:S(2)}, u32[]{:S(2)}) collective-permute-start(bf16[256,12,64]{0,2,1:T(8,128)(2,1)S(1)} %collective-permute-done.7), channel_id=1, source_target_pairs={{0,7},{1,0},{2,1},{3,2},{4,3},{5,4},{6,5},{7,6},{8,15},{9,8},{10,9... | collective-permute-start | bytes 1179656 | tf_op jit(solution)/shard_map/ppermute | solution.py:188
  146.6 9.3 %collective-permute-start.10 = (bf16[256,12,64]{0,2,1:T(8,128)(2,1)}, bf16[256,12,64]{0,2,1:T(8,128)(2,1)S(1)}, u32[]{:S(2)}, u32[]{:S(2)}) collective-permute-start(bf16[256,12,64]{0,2,1:T(8,128)(2,1)} %collective-permute-done.8), channel_id=1, source_target_pairs={{0,1},{1,2},{2,3},{3,4},{4,5},{5,6},{6,7},{7,0},{8,9},{9,10},{10,1... | collective-permute-start | bytes 1179656 | tf_op jit(solution)/shard_map/ppermute | solution.py:181
  156.7 64.1 %copy-start.4 = (bf16[1,256,768]{2,1,0:T(8,128)(2,1)S(1)}, bf16[1,256,768]{2,1,0:T(8,128)(2,1)}, u32[]{:S(2)}) copy-start(bf16[1,256,768]{2,1,0:T(8,128)(2,1)} %param.33) | copy-start | bytes 1179652
  220.7 13.4 %copy-start.17 = (f32[12,256]{1,0:T(8,128)}, f32[12,256]{1,0:T(8,128)S(1)}, u32[]{:S(2)}) copy-start(f32[12,256]{1,0:T(8,128)S(1)} %get-tuple-element.380) | copy-start | bytes 36868
  222.4 322.6 %reduce-scatter.9.cloned.1.call-start = ((), (), s32[]{:S(2)}) async-start(), calls=%async_computation.11 | async-start | bytes 5898240 | tf_op jit(solution)/shard_map/reduce_scatter | solution.py:289
  234.1 41.7 %copy-start.9 = (bf16[256,3072]{1,0:T(8,128)(2,1)}, bf16[256,3072]{1,0:T(8,128)(2,1)S(1)}, u32[]{:S(2)}) copy-start(bf16[256,3072]{1,0:T(8,128)(2,1)S(1)} %get-tuple-element.562) | copy-start | bytes 4718596
  253.7 291.4 %reduce-scatter.11.cloned.1.call-start = ((), (), s32[]{:S(2)}) async-start(), calls=%async_computation.12 | async-start | bytes 5898240 | tf_op jit(solution)/shard_map/reduce_scatter | solution.py:295
  279.4 299.9 %reduce-scatter.5.cloned.1.call-start = ((), (), s32[]{:S(2)}) async-start(), calls=%async_computation.9 | async-start | bytes 4423680 | tf_op jit(solution)/shard_map/reduce_scatter | solution.py:277
  283.0 247.1 %copy-start.29 = (f32[256,16]{0,1:T(8,128)S(1)}, f32[256,16]{0,1:T(8,128)}, u32[]{:S(2)}) copy-start(f32[256,16]{0,1:T(8,128)} %copy-done.28) | copy-start | bytes 49156
  291.6 9.3 %collective-permute-start.2 = (bf16[256,12,64]{0,2,1:T(8,128)(2,1)}, bf16[256,12,64]{0,2,1:T(8,128)(2,1)}, u32[]{:S(2)}, u32[]{:S(2)}) collective-permute-start(bf16[256,12,64]{0,2,1:T(8,128)(2,1)} %fusion.191), channel_id=1, source_target_pairs={{0,1},{1,2},{2,3},{3,4},{4,5},{5,6},{6,7},{7,0},{8,9},{9,10},{10,1... | collective-permute-start | bytes 1179656 | tf_op jit(solution)/shard_map/while/body/eval_jaxpr/ppermute | solution.py:16
  294.2 10.9 %collective-permute-start.3 = (bf16[256,12,64]{0,2,1:T(8,128)(2,1)}, bf16[256,12,64]{0,2,1:T(8,128)(2,1)}, u32[]{:S(2)}, u32[]{:S(2)}) collective-permute-start(bf16[256,12,64]{0,2,1:T(8,128)(2,1)} %fusion.192), channel_id=1, source_target_pairs={{0,1},{1,2},{2,3},{3,4},{4,5},{5,6},{6,7},{7,0},{8,9},{9,10},{10,1... | collective-permute-start | bytes 1179656 | tf_op jit(solution)/shard_map/while/body/eval_jaxpr/ppermute | solution.py:16
  295.7 13.7 %collective-permute-start = (bf16[256,12,64]{0,2,1:T(8,128)(2,1)S(1)}, bf16[256,12,64]{0,2,1:T(8,128)(2,1)}, u32[]{:S(2)}, u32[]{:S(2)}) collective-permute-start(bf16[256,12,64]{0,2,1:T(8,128)(2,1)S(1)} %copy.84), channel_id=1, source_target_pairs={{0,1},{1,2},{2,3},{3,4},{4,5},{5,6},{6,7},{7,0},{8,9},{9,10},{10,1... | collective-permute-start | bytes 1179656 | tf_op jit(solution)/shard_map/while/body/eval_jaxpr/ppermute | solution.py:16
  295.8 17.8 %collective-permute-start.1 = (bf16[256,12,64]{0,2,1:T(8,128)(2,1)}, bf16[256,12,64]{0,2,1:T(8,128)(2,1)}, u32[]{:S(2)}, u32[]{:S(2)}) collective-permute-start(bf16[256,12,64]{0,2,1:T(8,128)(2,1)} %copy.85), channel_id=1, source_target_pairs={{0,1},{1,2},{2,3},{3,4},{4,5},{5,6},{6,7},{7,0},{8,9},{9,10},{10,1... | collective-permute-start | bytes 1179656 | tf_op jit(solution)/shard_map/while/body/eval_jaxpr/ppermute | solution.py:16
  322.2 9.3 %collective-permute-start.2 = (bf16[256,12,64]{0,2,1:T(8,128)(2,1)}, bf16[256,12,64]{0,2,1:T(8,128)(2,1)}, u32[]{:S(2)}, u32[]{:S(2)}) collective-permute-start(bf16[256,12,64]{0,2,1:T(8,128)(2,1)} %fusion.191), channel_id=1, source_target_pairs={{0,1},{1,2},{2,3},{3,4},{4,5},{5,6},{6,7},{7,0},{8,9},{9,10},{10,1... | collective-permute-start | bytes 1179656 | tf_op jit(solution)/shard_map/while/body/eval_jaxpr/ppermute | solution.py:16
  324.9 10.8 %collective-permute-start.3 = (bf16[256,12,64]{0,2,1:T(8,128)(2,1)}, bf16[256,12,64]{0,2,1:T(8,128)(2,1)}, u32[]{:S(2)}, u32[]{:S(2)}) collective-permute-start(bf16[256,12,64]{0,2,1:T(8,128)(2,1)} %fusion.192), channel_id=1, source_target_pairs={{0,1},{1,2},{2,3},{3,4},{4,5},{5,6},{6,7},{7,0},{8,9},{9,10},{10,1... | collective-permute-start | bytes 1179656 | tf_op jit(solution)/shard_map/while/body/eval_jaxpr/ppermute | solution.py:16
  324.9 15.1 %collective-permute-start = (bf16[256,12,64]{0,2,1:T(8,128)(2,1)S(1)}, bf16[256,12,64]{0,2,1:T(8,128)(2,1)}, u32[]{:S(2)}, u32[]{:S(2)}) collective-permute-start(bf16[256,12,64]{0,2,1:T(8,128)(2,1)S(1)} %copy.84), channel_id=1, source_target_pairs={{0,1},{1,2},{2,3},{3,4},{4,5},{5,6},{6,7},{7,0},{8,9},{9,10},{10,1... | collective-permute-start | bytes 1179656 | tf_op jit(solution)/shard_map/while/body/eval_jaxpr/ppermute | solution.py:16
  324.9 19.3 %collective-permute-start.1 = (bf16[256,12,64]{0,2,1:T(8,128)(2,1)}, bf16[256,12,64]{0,2,1:T(8,128)(2,1)}, u32[]{:S(2)}, u32[]{:S(2)}) collective-permute-start(bf16[256,12,64]{0,2,1:T(8,128)(2,1)} %copy.85), channel_id=1, source_target_pairs={{0,1},{1,2},{2,3},{3,4},{4,5},{5,6},{6,7},{7,0},{8,9},{9,10},{10,1... | collective-permute-start | bytes 1179656 | tf_op jit(solution)/shard_map/while/body/eval_jaxpr/ppermute | solution.py:16
  352.8 9.3 %collective-permute-start.2 = (bf16[256,12,64]{0,2,1:T(8,128)(2,1)}, bf16[256,12,64]{0,2,1:T(8,128)(2,1)}, u32[]{:S(2)}, u32[]{:S(2)}) collective-permute-start(bf16[256,12,64]{0,2,1:T(8,128)(2,1)} %fusion.191), channel_id=1, source_target_pairs={{0,1},{1,2},{2,3},{3,4},{4,5},{5,6},{6,7},{7,0},{8,9},{9,10},{10,1... | collective-permute-start | bytes 1179656 | tf_op jit(solution)/shard_map/while/body/eval_jaxpr/ppermute | solution.py:16
  355.4 10.9 %collective-permute-start.3 = (bf16[256,12,64]{0,2,1:T(8,128)(2,1)}, bf16[256,12,64]{0,2,1:T(8,128)(2,1)}, u32[]{:S(2)}, u32[]{:S(2)}) collective-permute-start(bf16[256,12,64]{0,2,1:T(8,128)(2,1)} %fusion.192), channel_id=1, source_target_pairs={{0,1},{1,2},{2,3},{3,4},{4,5},{5,6},{6,7},{7,0},{8,9},{9,10},{10,1... | collective-permute-start | bytes 1179656 | tf_op jit(solution)/shard_map/while/body/eval_jaxpr/ppermute | solution.py:16
  355.4 15.1 %collective-permute-start = (bf16[256,12,64]{0,2,1:T(8,128)(2,1)S(1)}, bf16[256,12,64]{0,2,1:T(8,128)(2,1)}, u32[]{:S(2)}, u32[]{:S(2)}) collective-permute-start(bf16[256,12,64]{0,2,1:T(8,128)(2,1)S(1)} %copy.84), channel_id=1, source_target_pairs={{0,1},{1,2},{2,3},{3,4},{4,5},{5,6},{6,7},{7,0},{8,9},{9,10},{10,1... | collective-permute-start | bytes 1179656 | tf_op jit(solution)/shard_map/while/body/eval_jaxpr/ppermute | solution.py:16
  355.4 19.3 %collective-permute-start.1 = (bf16[256,12,64]{0,2,1:T(8,128)(2,1)}, bf16[256,12,64]{0,2,1:T(8,128)(2,1)}, u32[]{:S(2)}, u32[]{:S(2)}) collective-permute-start(bf16[256,12,64]{0,2,1:T(8,128)(2,1)} %copy.85), channel_id=1, source_target_pairs={{0,1},{1,2},{2,3},{3,4},{4,5},{5,6},{6,7},{7,0},{8,9},{9,10},{10,1... | collective-permute-start | bytes 1179656 | tf_op jit(solution)/shard_map/while/body/eval_jaxpr/ppermute | solution.py:16
  383.4 9.3 %collective-permute-start.2 = (bf16[256,12,64]{0,2,1:T(8,128)(2,1)}, bf16[256,12,64]{0,2,1:T(8,128)(2,1)}, u32[]{:S(2)}, u32[]{:S(2)}) collective-permute-start(bf16[256,12,64]{0,2,1:T(8,128)(2,1)} %fusion.191), channel_id=1, source_target_pairs={{0,1},{1,2},{2,3},{3,4},{4,5},{5,6},{6,7},{7,0},{8,9},{9,10},{10,1... | collective-permute-start | bytes 1179656 | tf_op jit(solution)/shard_map/while/body/eval_jaxpr/ppermute | solution.py:16
  386.1 10.8 %collective-permute-start.3 = (bf16[256,12,64]{0,2,1:T(8,128)(2,1)}, bf16[256,12,64]{0,2,1:T(8,128)(2,1)}, u32[]{:S(2)}, u32[]{:S(2)}) collective-permute-start(bf16[256,12,64]{0,2,1:T(8,128)(2,1)} %fusion.192), channel_id=1, source_target_pairs={{0,1},{1,2},{2,3},{3,4},{4,5},{5,6},{6,7},{7,0},{8,9},{9,10},{10,1... | collective-permute-start | bytes 1179656 | tf_op jit(solution)/shard_map/while/body/eval_jaxpr/ppermute | solution.py:16
  386.1 15.1 %collective-permute-start = (bf16[256,12,64]{0,2,1:T(8,128)(2,1)S(1)}, bf16[256,12,64]{0,2,1:T(8,128)(2,1)}, u32[]{:S(2)}, u32[]{:S(2)}) collective-permute-start(bf16[256,12,64]{0,2,1:T(8,128)(2,1)S(1)} %copy.84), channel_id=1, source_target_pairs={{0,1},{1,2},{2,3},{3,4},{4,5},{5,6},{6,7},{7,0},{8,9},{9,10},{10,1... | collective-permute-start | bytes 1179656 | tf_op jit(solution)/shard_map/while/body/eval_jaxpr/ppermute | solution.py:16
  386.1 19.3 %collective-permute-start.1 = (bf16[256,12,64]{0,2,1:T(8,128)(2,1)}, bf16[256,12,64]{0,2,1:T(8,128)(2,1)}, u32[]{:S(2)}, u32[]{:S(2)}) collective-permute-start(bf16[256,12,64]{0,2,1:T(8,128)(2,1)} %copy.85), channel_id=1, source_target_pairs={{0,1},{1,2},{2,3},{3,4},{4,5},{5,6},{6,7},{7,0},{8,9},{9,10},{10,1... | collective-permute-start | bytes 1179656 | tf_op jit(solution)/shard_map/while/body/eval_jaxpr/ppermute | solution.py:16
  414.1 9.3 %collective-permute-start.2 = (bf16[256,12,64]{0,2,1:T(8,128)(2,1)}, bf16[256,12,64]{0,2,1:T(8,128)(2,1)}, u32[]{:S(2)}, u32[]{:S(2)}) collective-permute-start(bf16[256,12,64]{0,2,1:T(8,128)(2,1)} %fusion.191), channel_id=1, source_target_pairs={{0,1},{1,2},{2,3},{3,4},{4,5},{5,6},{6,7},{7,0},{8,9},{9,10},{10,1... | collective-permute-start | bytes 1179656 | tf_op jit(solution)/shard_map/while/body/eval_jaxpr/ppermute | solution.py:16
  416.7 10.9 %collective-permute-start.3 = (bf16[256,12,64]{0,2,1:T(8,128)(2,1)}, bf16[256,12,64]{0,2,1:T(8,128)(2,1)}, u32[]{:S(2)}, u32[]{:S(2)}) collective-permute-start(bf16[256,12,64]{0,2,1:T(8,128)(2,1)} %fusion.192), channel_id=1, source_target_pairs={{0,1},{1,2},{2,3},{3,4},{4,5},{5,6},{6,7},{7,0},{8,9},{9,10},{10,1... | collective-permute-start | bytes 1179656 | tf_op jit(solution)/shard_map/while/body/eval_jaxpr/ppermute | solution.py:16
  416.7 15.1 %collective-permute-start = (bf16[256,12,64]{0,2,1:T(8,128)(2,1)S(1)}, bf16[256,12,64]{0,2,1:T(8,128)(2,1)}, u32[]{:S(2)}, u32[]{:S(2)}) collective-permute-start(bf16[256,12,64]{0,2,1:T(8,128)(2,1)S(1)} %copy.84), channel_id=1, source_target_pairs={{0,1},{1,2},{2,3},{3,4},{4,5},{5,6},{6,7},{7,0},{8,9},{9,10},{10,1... | collective-permute-start | bytes 1179656 | tf_op jit(solution)/shard_map/while/body/eval_jaxpr/ppermute | solution.py:16
  416.7 19.3 %collective-permute-start.1 = (bf16[256,12,64]{0,2,1:T(8,128)(2,1)}, bf16[256,12,64]{0,2,1:T(8,128)(2,1)}, u32[]{:S(2)}, u32[]{:S(2)}) collective-permute-start(bf16[256,12,64]{0,2,1:T(8,128)(2,1)} %copy.85), channel_id=1, source_target_pairs={{0,1},{1,2},{2,3},{3,4},{4,5},{5,6},{6,7},{7,0},{8,9},{9,10},{10,1... | collective-permute-start | bytes 1179656 | tf_op jit(solution)/shard_map/while/body/eval_jaxpr/ppermute | solution.py:16
  444.7 9.3 %collective-permute-start.2 = (bf16[256,12,64]{0,2,1:T(8,128)(2,1)}, bf16[256,12,64]{0,2,1:T(8,128)(2,1)}, u32[]{:S(2)}, u32[]{:S(2)}) collective-permute-start(bf16[256,12,64]{0,2,1:T(8,128)(2,1)} %fusion.191), channel_id=1, source_target_pairs={{0,1},{1,2},{2,3},{3,4},{4,5},{5,6},{6,7},{7,0},{8,9},{9,10},{10,1... | collective-permute-start | bytes 1179656 | tf_op jit(solution)/shard_map/while/body/eval_jaxpr/ppermute | solution.py:16
  447.3 10.9 %collective-permute-start.3 = (bf16[256,12,64]{0,2,1:T(8,128)(2,1)}, bf16[256,12,64]{0,2,1:T(8,128)(2,1)}, u32[]{:S(2)}, u32[]{:S(2)}) collective-permute-start(bf16[256,12,64]{0,2,1:T(8,128)(2,1)} %fusion.192), channel_id=1, source_target_pairs={{0,1},{1,2},{2,3},{3,4},{4,5},{5,6},{6,7},{7,0},{8,9},{9,10},{10,1... | collective-permute-start | bytes 1179656 | tf_op jit(solution)/shard_map/while/body/eval_jaxpr/ppermute | solution.py:16
  447.3 15.1 %collective-permute-start = (bf16[256,12,64]{0,2,1:T(8,128)(2,1)S(1)}, bf16[256,12,64]{0,2,1:T(8,128)(2,1)}, u32[]{:S(2)}, u32[]{:S(2)}) collective-permute-start(bf16[256,12,64]{0,2,1:T(8,128)(2,1)S(1)} %copy.84), channel_id=1, source_target_pairs={{0,1},{1,2},{2,3},{3,4},{4,5},{5,6},{6,7},{7,0},{8,9},{9,10},{10,1... | collective-permute-start | bytes 1179656 | tf_op jit(solution)/shard_map/while/body/eval_jaxpr/ppermute | solution.py:16
  447.3 19.3 %collective-permute-start.1 = (bf16[256,12,64]{0,2,1:T(8,128)(2,1)}, bf16[256,12,64]{0,2,1:T(8,128)(2,1)}, u32[]{:S(2)}, u32[]{:S(2)}) collective-permute-start(bf16[256,12,64]{0,2,1:T(8,128)(2,1)} %copy.85), channel_id=1, source_target_pairs={{0,1},{1,2},{2,3},{3,4},{4,5},{5,6},{6,7},{7,0},{8,9},{9,10},{10,1... | collective-permute-start | bytes 1179656 | tf_op jit(solution)/shard_map/while/body/eval_jaxpr/ppermute | solution.py:16
  475.3 9.3 %collective-permute-start.2 = (bf16[256,12,64]{0,2,1:T(8,128)(2,1)}, bf16[256,12,64]{0,2,1:T(8,128)(2,1)}, u32[]{:S(2)}, u32[]{:S(2)}) collective-permute-start(bf16[256,12,64]{0,2,1:T(8,128)(2,1)} %fusion.191), channel_id=1, source_target_pairs={{0,1},{1,2},{2,3},{3,4},{4,5},{5,6},{6,7},{7,0},{8,9},{9,10},{10,1... | collective-permute-start | bytes 1179656 | tf_op jit(solution)/shard_map/while/body/eval_jaxpr/ppermute | solution.py:16
  477.9 10.9 %collective-permute-start.3 = (bf16[256,12,64]{0,2,1:T(8,128)(2,1)}, bf16[256,12,64]{0,2,1:T(8,128)(2,1)}, u32[]{:S(2)}, u32[]{:S(2)}) collective-permute-start(bf16[256,12,64]{0,2,1:T(8,128)(2,1)} %fusion.192), channel_id=1, source_target_pairs={{0,1},{1,2},{2,3},{3,4},{4,5},{5,6},{6,7},{7,0},{8,9},{9,10},{10,1... | collective-permute-start | bytes 1179656 | tf_op jit(solution)/shard_map/while/body/eval_jaxpr/ppermute | solution.py:16
  477.9 15.1 %collective-permute-start = (bf16[256,12,64]{0,2,1:T(8,128)(2,1)S(1)}, bf16[256,12,64]{0,2,1:T(8,128)(2,1)}, u32[]{:S(2)}, u32[]{:S(2)}) collective-permute-start(bf16[256,12,64]{0,2,1:T(8,128)(2,1)S(1)} %copy.84), channel_id=1, source_target_pairs={{0,1},{1,2},{2,3},{3,4},{4,5},{5,6},{6,7},{7,0},{8,9},{9,10},{10,1... | collective-permute-start | bytes 1179656 | tf_op jit(solution)/shard_map/while/body/eval_jaxpr/ppermute | solution.py:16
  477.9 19.3 %collective-permute-start.1 = (bf16[256,12,64]{0,2,1:T(8,128)(2,1)}, bf16[256,12,64]{0,2,1:T(8,128)(2,1)}, u32[]{:S(2)}, u32[]{:S(2)}) collective-permute-start(bf16[256,12,64]{0,2,1:T(8,128)(2,1)} %copy.85), channel_id=1, source_target_pairs={{0,1},{1,2},{2,3},{3,4},{4,5},{5,6},{6,7},{7,0},{8,9},{9,10},{10,1... | collective-permute-start | bytes 1179656 | tf_op jit(solution)/shard_map/while/body/eval_jaxpr/ppermute | solution.py:16
  505.8 9.3 %collective-permute-start.2 = (bf16[256,12,64]{0,2,1:T(8,128)(2,1)}, bf16[256,12,64]{0,2,1:T(8,128)(2,1)}, u32[]{:S(2)}, u32[]{:S(2)}) collective-permute-start(bf16[256,12,64]{0,2,1:T(8,128)(2,1)} %fusion.191), channel_id=1, source_target_pairs={{0,1},{1,2},{2,3},{3,4},{4,5},{5,6},{6,7},{7,0},{8,9},{9,10},{10,1... | collective-permute-start | bytes 1179656 | tf_op jit(solution)/shard_map/while/body/eval_jaxpr/ppermute | solution.py:16
  508.5 10.9 %collective-permute-start.3 = (bf16[256,12,64]{0,2,1:T(8,128)(2,1)}, bf16[256,12,64]{0,2,1:T(8,128)(2,1)}, u32[]{:S(2)}, u32[]{:S(2)}) collective-permute-start(bf16[256,12,64]{0,2,1:T(8,128)(2,1)} %fusion.192), channel_id=1, source_target_pairs={{0,1},{1,2},{2,3},{3,4},{4,5},{5,6},{6,7},{7,0},{8,9},{9,10},{10,1... | collective-permute-start | bytes 1179656 | tf_op jit(solution)/shard_map/while/body/eval_jaxpr/ppermute | solution.py:16
  508.5 15.1 %collective-permute-start = (bf16[256,12,64]{0,2,1:T(8,128)(2,1)S(1)}, bf16[256,12,64]{0,2,1:T(8,128)(2,1)}, u32[]{:S(2)}, u32[]{:S(2)}) collective-permute-start(bf16[256,12,64]{0,2,1:T(8,128)(2,1)S(1)} %copy.84), channel_id=1, source_target_pairs={{0,1},{1,2},{2,3},{3,4},{4,5},{5,6},{6,7},{7,0},{8,9},{9,10},{10,1... | collective-permute-start | bytes 1179656 | tf_op jit(solution)/shard_map/while/body/eval_jaxpr/ppermute | solution.py:16
  508.5 19.3 %collective-permute-start.1 = (bf16[256,12,64]{0,2,1:T(8,128)(2,1)}, bf16[256,12,64]{0,2,1:T(8,128)(2,1)}, u32[]{:S(2)}, u32[]{:S(2)}) collective-permute-start(bf16[256,12,64]{0,2,1:T(8,128)(2,1)} %copy.85), channel_id=1, source_target_pairs={{0,1},{1,2},{2,3},{3,4},{4,5},{5,6},{6,7},{7,0},{8,9},{9,10},{10,1... | collective-permute-start | bytes 1179656 | tf_op jit(solution)/shard_map/while/body/eval_jaxpr/ppermute | solution.py:16
  534.8 132.9 %all-reduce.20.cloned.1.call-start = ((), (), s32[]{:S(2)}) async-start(), calls=%async_computation.13 | async-start | bytes 7077888 | tf_op jit(solution)/shard_map/psum | solution.py:312
  545.0 36.3 %copy-start.45 = (bf16[3072]{0:T(1024)(128)(2,1)S(1)}, bf16[3072]{0:T(1024)(128)(2,1)}, u32[]{:S(2)}) copy-start(bf16[3072]{0:T(1024)(128)(2,1)} %get-tuple-element.588) | copy-start | bytes 18436
  545.0 71.0 %copy-start.10 = (bf16[256,3072]{1,0:T(8,128)(2,1)S(1)}, bf16[256,3072]{1,0:T(8,128)(2,1)}, u32[]{:S(2)}) copy-start(bf16[256,3072]{1,0:T(8,128)(2,1)} %copy-done.9) | copy-start | bytes 4718596
  613.7 60.9 %copy-start.46 = (f32[192]{0:T(256)}, f32[192]{0:T(256)S(1)}, u32[]{:S(2)}) copy-start(f32[192]{0:T(256)S(1)} %convert_element_type.269) | copy-start | bytes 2308
  (74 other events, 182.5 us)
Sparse Core Ops, SparseCore 0:
  9.9 50.0 all-gather.7
  69.1 57.2 all-gather.9
  128.3 54.8 all-gather.13
  184.8 57.0 all-gather.15
  243.6 27.7 all-gather.11
  274.7 28.5 reduce-scatter.6
  306.3 57.0 reduce-scatter.8
  366.4 57.0 reduce-scatter.10
  534.9 44.3 reduce-scatter.4
  581.8 85.8 all-reduce.19
